TPU v7x, 256 devices: a whole 4x4x8 slice. The times are simulated.
256 devices in a mesh: dp: 4 (over z_lo), feat: 64 (over y, z_hi, x, core).
Axes of the slice: x: 4, y: 4, z: 8 (z_hi: 2, z_lo: 4; z = z_hi * 4 + z_lo), core: 2. Of those that a mesh axis runs over, the one named last changes fastest.
Arguments:
- features: bfloat16 [1024, 32768], P('dp', 'feat'), may hold values from -6 to 6
- diag_first: bfloat16 [128, 256, 256], P('feat'), may hold values from -0.125 to 0.125
- part_first: bfloat16 [7, 128, 256, 256], P(None, 'feat'), may hold values from -0.125 to 0.125
- bias_first: bfloat16 [32768], P('feat'), may hold values from -3 to 3
- diag_second: bfloat16 [128, 256, 256], P('feat'), may hold values from -0.125 to 0.125
- part_second: bfloat16 [7, 128, 256, 256], P(None, 'feat'), may hold values from -0.125 to 0.125
- section_bit: int32 [7], replicated, may hold values from 0 to 6, each once
- grad_out: bfloat16 [1024, 32768], P('dp', 'feat'), may hold values from -6 to 6
Outputs:
- output: bfloat16 [1024, 32768], P('dp', 'feat')
- grad_features: bfloat16 [1024, 32768], P('dp', 'feat')
- grad_diag_first: bfloat16 [128, 256, 256], P('feat')
- grad_part_first: bfloat16 [7, 128, 256, 256], P(None, 'feat')
- grad_bias_first: bfloat16 [32768], P('feat')
- grad_diag_second: bfloat16 [128, 256, 256], P('feat')
- grad_part_second: bfloat16 [7, 128, 256, 256], P(None, 'feat')
Inputs may be any that keep to these rules, and one draw needn't show every extreme that they name: section_bit holds each of 0 to 6 exactly once.
All inputs are finite; a program needn't handle non-finite values.
Results may differ from a plain program's by a relative error of at most 0.019.
Values may be sent and summed in bfloat16 or wider, within the bound.
No kernel may reach another device: no remote copies, remote signals or barrier semaphores. Data moves between devices by JAX's collectives and lax.ppermute only.
A program may use at most 64 MiB of HBM per device.

v0:
```python
import jax
import jax.numpy as jnp
from jax import lax
from jax.sharding import PartitionSpec as P

SECTIONS = 7
BS = 256


def from_partner(value, axis, stride):
    mask = 2**stride
    pairs = [(source, source ^ mask) for source in range(lax.axis_size(axis))]
    return lax.ppermute(value, axis, pairs)


def factor_of(section_bit, level):
    order = jnp.arange(section_bit.shape[0], dtype=jnp.int32)
    return jnp.sum(jnp.where(section_bit == level, order, 0))


def flip_local(item, level):
    stride = 1 << level
    shape = item.shape
    folded = item.reshape(shape[0], shape[1] // (2 * stride), 2, stride, shape[2])
    return folded[:, :, ::-1].reshape(shape)


def partners(value, level, local_bits, fetch):
    if level < local_bits:
        return flip_local(value, level)
    return fetch(value, level - local_bits)


def forward_mix(blocks, diagonal, partner, section_bit, local_bits, fetch):
    total = jnp.einsum("tib,ibc->tic", blocks, diagonal, preferred_element_type=jnp.float32)
    others = []
    for level in range(SECTIONS):
        other = partners(blocks, level, local_bits, fetch)
        weight = lax.dynamic_index_in_dim(partner, factor_of(section_bit, level), 0, keepdims=False)
        total = total + jnp.einsum(
            "tib,ibc->tic", other, weight, preferred_element_type=jnp.float32
        )
        others.append(other)
    return (total, others)


def backward_mix(grad, diagonal, partner, section_bit, local_bits):
    total = jnp.einsum("tic,ibc->tib", grad, diagonal, preferred_element_type=jnp.float32)
    for level in range(SECTIONS):
        weight = lax.dynamic_index_in_dim(partner, factor_of(section_bit, level), 0, keepdims=False)
        if level < local_bits:
            product_term = jnp.einsum(
                "tic,ibc->tib", grad, weight, preferred_element_type=jnp.float32
            )
            total = total + flip_local(product_term, level)
        else:
            product_term = jnp.einsum(
                "tic,ibc->tib", grad, weight, preferred_element_type=jnp.float32
            )
            total = total + from_partner(
                product_term.astype(jnp.bfloat16), "feat", level - local_bits
            ).astype(product_term.dtype)
    return total


def weight_partials(blocks, others, grad, section_bit):
    diag_grad = jnp.einsum("tib,tic->ibc", blocks, grad, preferred_element_type=jnp.float32)
    pieces = [
        jnp.einsum("tib,tic->ibc", other, grad, preferred_element_type=jnp.float32)
        for other in others
    ]
    stacked = jnp.stack(pieces)
    return (diag_grad, jnp.take(stacked, section_bit, axis=0))


def on_device(
    features, diag_first, part_first, bias_first, diag_second, part_second, section_bit, grad_out
):
    rows = features.shape[0]
    blocks_here = features.shape[1] // BS
    local_bits = blocks_here.bit_length() - 1
    blocks = features.reshape(rows, blocks_here, BS)

    def fetch_forward(value, device_bit):
        return from_partner(value, "feat", device_bit)

    pre_sum, input_others = forward_mix(
        blocks, diag_first, part_first, section_bit, local_bits, fetch_forward
    )
    pre = pre_sum + bias_first.reshape(blocks_here, BS).astype(jnp.float32)
    hidden = jax.nn.gelu(pre, approximate=True).astype(jnp.bfloat16)
    out_sum, hidden_others = forward_mix(
        hidden, diag_second, part_second, section_bit, local_bits, fetch_forward
    )
    output = out_sum.astype(jnp.bfloat16).reshape(rows, -1)
    grad_blocks = grad_out.reshape(rows, blocks_here, BS)
    grad_hidden = backward_mix(grad_blocks, diag_second, part_second, section_bit, local_bits)
    _, pull = jax.vjp(lambda value: jax.nn.gelu(value, approximate=True), pre)
    grad_pre = pull(grad_hidden)[0].astype(jnp.bfloat16)
    grad_in = backward_mix(grad_pre, diag_first, part_first, section_bit, local_bits)
    second_diag, second_part = weight_partials(hidden, hidden_others, grad_blocks, section_bit)
    first_diag, first_part = weight_partials(blocks, input_others, grad_pre, section_bit)
    bias_partial = jnp.sum(grad_pre.astype(jnp.float32), axis=0).reshape(-1)
    first_diag, first_part, bias_total, second_diag, second_part = (
        lax.psum(first_diag.astype(jnp.bfloat16), "dp").astype(jnp.float32),
        lax.psum(first_part.astype(jnp.bfloat16), "dp").astype(jnp.float32),
        lax.psum(bias_partial.astype(jnp.bfloat16), "dp").astype(jnp.float32),
        lax.psum(second_diag.astype(jnp.bfloat16), "dp").astype(jnp.float32),
        lax.psum(second_part.astype(jnp.bfloat16), "dp").astype(jnp.float32),
    )
    grad_in = grad_in.astype(jnp.bfloat16).reshape(rows, -1)
    return (
        output,
        grad_in,
        first_diag.astype(jnp.bfloat16),
        first_part.astype(jnp.bfloat16),
        bias_total.astype(jnp.bfloat16),
        second_diag.astype(jnp.bfloat16),
        second_part.astype(jnp.bfloat16),
    )


def solution(mesh):
    in_specs = (
        P("dp", "feat"),
        P("feat", None, None),
        P(None, "feat", None, None),
        P("feat"),
        P("feat", None, None),
        P(None, "feat", None, None),
        P(),
        P("dp", "feat"),
    )
    out_specs = (
        P("dp", "feat"),
        P("dp", "feat"),
        P("feat", None, None),
        P(None, "feat", None, None),
        P("feat"),
        P("feat", None, None),
        P(None, "feat", None, None),
    )
    return jax.shard_map(
        on_device, mesh=mesh, in_specs=in_specs, out_specs=out_specs, check_vma=False
    )
```

profile of v0, /device:TPU:1, one launch (start us, length us, event | category | flops | bytes accessed | tf_op | source)
XLA Modules:
  0.0 318.6 jit_solution(5711974967249858122)
XLA Ops:
  9.3 3.7 %collective-permute-start.5 = (bf16[256,2,256]{2,0,1:T(8,128)(2,1)}, bf16[256,2,256]{2,0,1:T(8,128)(2,1)}, u32[]{:S(2)}, u32[]{:S(2)}) collective-permute-start(bf16[256,2,256]{2,0,1:T(8,128)(2,1)} %copy.77), channel_id=1, source_target_pairs={{0,32},{1,33},{2,34},{3,35},{4,36},{5,37},{6,38},{7,39},{8,40},{9,... | collective-permute-start | bytes 786440 | tf_op jit(solution)/shard_map/ppermute | solution.py:13
  13.5 6.9 %collective-permute-start.3 = (bf16[256,2,256]{2,0,1:T(8,128)(2,1)}, bf16[256,2,256]{2,0,1:T(8,128)(2,1)}, u32[]{:S(2)}, u32[]{:S(2)}) collective-permute-start(bf16[256,2,256]{2,0,1:T(8,128)(2,1)} %copy.77), channel_id=1, source_target_pairs={{0,8},{1,9},{2,10},{3,11},{4,12},{5,13},{6,14},{7,15},{8,0},{9,1},... | collective-permute-start | bytes 786440 | tf_op jit(solution)/shard_map/ppermute | solution.py:13
  20.4 2.7 collective-permute-start.2
  37.5 1.9 fusion.43
  42.0 1.9 fusion.41
  44.6 1.9 fusion.40
  51.6 2.0 convolution_bitcast_fusion.1
  56.6 2.1 collective-permute-start
  73.4 3.4 %collective-permute-start.11 = (bf16[256,2,256]{2,0,1:T(8,128)(2,1)S(1)}, bf16[256,2,256]{2,0,1:T(8,128)(2,1)}, u32[]{:S(2)}, u32[]{:S(2)}) collective-permute-start(bf16[256,2,256]{2,0,1:T(8,128)(2,1)S(1)} %get-tuple-element.34), channel_id=1, source_target_pairs={{0,32},{1,33},{2,34},{3,35},{4,36},{5,37},{6,38},{7,39},{8,40},{9,... | collective-permute-start | bytes 786440 | tf_op jit(solution)/shard_map/ppermute | solution.py:13
  78.1 2.6 collective-permute-start.9
  82.5 2.2 collective-permute-start.6
  84.7 2.5 fusion.183
  90.2 1.9 fusion.11
  92.1 1.9 fusion.10
  94.0 1.9 fusion.9
  96.0 1.9 fusion.8
  97.9 1.9 fusion.7
  99.8 3.4 %gather_fusion = bf16[7,2,256,256]{2,3,1,0:T(8,128)(2,1)} fusion(bf16[7,2,256,256]{2,3,1,0:T(8,128)(2,1)} %fusion.7, s32[1024]{0:T(1024)S(1)} %pad_clamp_fusion), kind=kCustom, calls=%fused_computation.clone | custom fusion | bytes 3670044 | tf_op jit(solution)/shard_map/jit(_take)/gather | solution.py:73
  103.3 3.4 %select_convert_fusion.1 = bf16[7,2,256,256]{2,3,1,0:T(8,128)(2,1)} fusion(bf16[7,2,256,256]{2,3,1,0:T(8,128)(2,1)} %gather_fusion, pred[7]{0:T(512)(128)(4,1)S(1)} %compare_and_fusion), kind=kLoop, calls=%fused_computation.3 | loop fusion | flops 917504 | bytes 3670023 | tf_op jit(solution)/shard_map/convert_element_type | solution.py:106
  109.7 1.9 fusion.4
  111.6 6.5 %collective-permute-done.8 = bf16[256,2,256]{2,0,1:T(8,128)(2,1)S(1)} collective-permute-done((bf16[256,2,256]{2,0,1:T(8,128)(2,1)S(1)}, bf16[256,2,256]{2,0,1:T(8,128)(2,1)S(1)}, u32[]{:S(2)}, u32[]{:S(2)}) %collective-permute-start.8) | collective-permute-done | bytes 262176 | tf_op jit(solution)/shard_map/ppermute | solution.py:13
  119.1 1.9 fusion.2
  121.1 1.9 fusion.1
  123.0 1.9 fusion
  124.9 3.4 %gather_fusion.1 = bf16[7,2,256,256]{3,2,1,0:T(8,128)(2,1)} fusion(bf16[7,2,256,256]{3,2,1,0:T(8,128)(2,1)} %fusion, s32[1024]{0:T(1024)S(1)} %pad_clamp_fusion), kind=kCustom, calls=%fused_computation.1.clone | custom fusion | bytes 3670044 | tf_op jit(solution)/shard_map/jit(_take)/gather | solution.py:73
  128.3 3.4 %select_convert_fusion = bf16[7,2,256,256]{3,2,1,0:T(8,128)(2,1)} fusion(bf16[7,2,256,256]{3,2,1,0:T(8,128)(2,1)} %gather_fusion.1, pred[7]{0:T(512)(128)(4,1)S(1)} %compare_and_fusion), kind=kLoop, calls=%fused_computation.2 | loop fusion | flops 917504 | bytes 3670023 | tf_op jit(solution)/shard_map/convert_element_type | solution.py:109
  132.8 2.8 collective-permute-start.23
  137.5 4.2 %collective-permute-start.21 = (bf16[256,2,256]{0,2,1:T(8,128)(2,1)}, bf16[256,2,256]{0,2,1:T(8,128)(2,1)}, u32[]{:S(2)}, u32[]{:S(2)}) collective-permute-start(bf16[256,2,256]{0,2,1:T(8,128)(2,1)} %fusion.34), channel_id=1, source_target_pairs={{0,8},{1,9},{2,10},{3,11},{4,12},{5,13},{6,14},{7,15},{8,0},{9,1},... | collective-permute-start | bytes 786440 | tf_op jit(solution)/shard_map/ppermute | solution.py:13
  145.4 26.2 %psum.37 = bf16[512]{0:T(512)(128)(2,1)} all-reduce(bf16[512]{0:T(512)(128)(2,1)S(1)} %bitcast.349), channel_id=1, replica_groups=mesh['dp'=4,'feat'=64] {'dp'}, use_global_device_ids=true, to_apply=%region_10.12 | all-reduce | flops 512 | bytes 2048 | tf_op jit(solution)/shard_map/psum | solution.py:107
  184.6 118.3 %all-reduce.3.cloned.1.call-done = (bf16[2,256,256]{1,2,0:T(8,128)(2,1)}, bf16[7,2,256,256]{2,3,1,0:T(8,128)(2,1)}, bf16[2,256,256]{2,1,0:T(8,128)(2,1)}, bf16[7,2,256,256]{3,2,1,0:T(8,128)(2,1)}) async-done(((bf16[2,256,256]{1,2,0:T(8,128)(2,1)}, bf16[7,2,256,256]{2,3,1,0:T(8,128)(2,1)}, bf16[2,256,256]{2,1,0:T(8,128)(2,1)}, bf16[7,2,256,256]{3,2,1,0:T(8,128)(2,1)}), (bf16[2,256,256]{1,2,0:T(8,128)(2,1)}, ...) | async-done | bytes 4194320 | tf_op jit(solution)/shard_map/psum | solution.py:105
  304.7 3.6 %copy.141 = bf16[7,2,256,256]{3,2,1,0:T(8,128)(2,1)} copy(bf16[7,2,256,256]{2,3,1,0:T(8,128)(2,1)} %get-tuple-element.30) | data formatting | bytes 3670016
  308.9 2.9 copy.274
  (127 shorter events, 61.2 us)
Async XLA Ops:
  7.2 46.5 %copy-start = (bf16[7,2,256,256]{3,2,1,0:T(8,128)(2,1)S(1)}, bf16[7,2,256,256]{3,2,1,0:T(8,128)(2,1)}, u32[]{:S(2)}) copy-start(bf16[7,2,256,256]{3,2,1,0:T(8,128)(2,1)} %param.12) | copy-start | bytes 5505028
  7.2 30.3 %copy-start.1 = (bf16[256,512]{1,0:T(8,128)(2,1)S(1)}, bf16[256,512]{1,0:T(8,128)(2,1)}, u32[]{:S(2)}) copy-start(bf16[256,512]{1,0:T(8,128)(2,1)} %param.17) | copy-start | bytes 786436
  7.2 295.7 %all-reduce.3.cloned.1.call-start = ((), (), s32[]{:S(2)}) async-start(), calls=%async_computation | async-start | bytes 8388608 | tf_op jit(solution)/shard_map/psum | solution.py:105
  9.3 47.3 %collective-permute-start.5 = (bf16[256,2,256]{2,0,1:T(8,128)(2,1)}, bf16[256,2,256]{2,0,1:T(8,128)(2,1)}, u32[]{:S(2)}, u32[]{:S(2)}) collective-permute-start(bf16[256,2,256]{2,0,1:T(8,128)(2,1)} %copy.77), channel_id=1, source_target_pairs={{0,32},{1,33},{2,34},{3,35},{4,36},{5,37},{6,38},{7,39},{8,40},{9,... | collective-permute-start | bytes 786440 | tf_op jit(solution)/shard_map/ppermute | solution.py:13
  13.1 46.8 %collective-permute-start.4 = (bf16[256,2,256]{2,0,1:T(8,128)(2,1)}, bf16[256,2,256]{2,0,1:T(8,128)(2,1)}, u32[]{:S(2)}, u32[]{:S(2)}) collective-permute-start(bf16[256,2,256]{2,0,1:T(8,128)(2,1)} %copy.77), channel_id=1, source_target_pairs={{0,16},{1,17},{2,18},{3,19},{4,20},{5,21},{6,22},{7,23},{8,24},{9,... | collective-permute-start | bytes 786440 | tf_op jit(solution)/shard_map/ppermute | solution.py:13
  13.5 49.2 %collective-permute-start.3 = (bf16[256,2,256]{2,0,1:T(8,128)(2,1)}, bf16[256,2,256]{2,0,1:T(8,128)(2,1)}, u32[]{:S(2)}, u32[]{:S(2)}) collective-permute-start(bf16[256,2,256]{2,0,1:T(8,128)(2,1)} %copy.77), channel_id=1, source_target_pairs={{0,8},{1,9},{2,10},{3,11},{4,12},{5,13},{6,14},{7,15},{8,0},{9,1},... | collective-permute-start | bytes 786440 | tf_op jit(solution)/shard_map/ppermute | solution.py:13
  20.4 43.7 %collective-permute-start.2 = (bf16[256,2,256]{2,0,1:T(8,128)(2,1)}, bf16[256,2,256]{2,0,1:T(8,128)(2,1)}, u32[]{:S(2)}, u32[]{:S(2)}) collective-permute-start(bf16[256,2,256]{2,0,1:T(8,128)(2,1)} %copy.77), channel_id=1, source_target_pairs={{0,4},{1,5},{2,6},{3,7},{4,0},{5,1},{6,2},{7,3},{8,12},{9,13},{10,... | collective-permute-start | bytes 786440 | tf_op jit(solution)/shard_map/ppermute | solution.py:13
  23.1 42.2 %collective-permute-start.1 = (bf16[256,2,256]{2,0,1:T(8,128)(2,1)}, bf16[256,2,256]{2,0,1:T(8,128)(2,1)}, u32[]{:S(2)}, u32[]{:S(2)}) collective-permute-start(bf16[256,2,256]{2,0,1:T(8,128)(2,1)} %copy.77), channel_id=1, source_target_pairs={{0,2},{1,3},{2,0},{3,1},{4,6},{5,7},{6,4},{7,5},{8,10},{9,11},{10,... | collective-permute-start | bytes 786440 | tf_op jit(solution)/shard_map/ppermute | solution.py:13
  49.1 5.6 %copy-start.15 = (bf16[512]{0:T(512)(128)(2,1)S(1)}, bf16[512]{0:T(512)(128)(2,1)}, u32[]{:S(2)}) copy-start(bf16[512]{0:T(512)(128)(2,1)} %param.13) | copy-start | bytes 3076
  56.6 11.7 %collective-permute-start = (bf16[256,2,256]{2,0,1:T(8,128)(2,1)}, bf16[256,2,256]{2,0,1:T(8,128)(2,1)S(1)}, u32[]{:S(2)}, u32[]{:S(2)}) collective-permute-start(bf16[256,2,256]{2,0,1:T(8,128)(2,1)} %copy.77), channel_id=1, source_target_pairs={{0,1},{1,0},{2,3},{3,2},{4,5},{5,4},{6,7},{7,6},{8,9},{9,8},{10,11... | collective-permute-start | bytes 786440 | tf_op jit(solution)/shard_map/ppermute | solution.py:13
  59.9 9.5 %collective-permute-start.17 = (bf16[256,2,256]{2,0,1:T(8,128)(2,1)S(1)}, bf16[256,2,256]{2,0,1:T(8,128)(2,1)S(1)}, u32[]{:S(2)}, u32[]{:S(2)}) collective-permute-start(bf16[256,2,256]{2,0,1:T(8,128)(2,1)S(1)} %copy-done.14), channel_id=1, source_target_pairs={{0,32},{1,33},{2,34},{3,35},{4,36},{5,37},{6,38},{7,39},{8,40},{9,... | collective-permute-start | bytes 786440 | tf_op jit(solution)/shard_map/ppermute | solution.py:13
  62.7 8.6 %copy-start.3 = (f32[2,256,256]{1,2,0:T(8,128)S(1)}, f32[2,256,256]{1,2,0:T(8,128)}, u32[]{:S(2)}) copy-start(f32[2,256,256]{1,2,0:T(8,128)} %convolution_add_fusion.1) | copy-start | bytes 1572868
  62.7 10.7 %collective-permute-start.16 = (bf16[256,2,256]{2,0,1:T(8,128)(2,1)}, bf16[256,2,256]{2,0,1:T(8,128)(2,1)}, u32[]{:S(2)}, u32[]{:S(2)}) collective-permute-start(bf16[256,2,256]{2,0,1:T(8,128)(2,1)} %fusion.42), channel_id=1, source_target_pairs={{0,16},{1,17},{2,18},{3,19},{4,20},{5,21},{6,22},{7,23},{8,24},{9,... | collective-permute-start | bytes 786440 | tf_op jit(solution)/shard_map/ppermute | solution.py:13
  64.1 13.0 %collective-permute-start.15 = (bf16[256,2,256]{2,0,1:T(8,128)(2,1)}, bf16[256,2,256]{2,0,1:T(8,128)(2,1)}, u32[]{:S(2)}, u32[]{:S(2)}) collective-permute-start(bf16[256,2,256]{2,0,1:T(8,128)(2,1)} %fusion.41), channel_id=1, source_target_pairs={{0,8},{1,9},{2,10},{3,11},{4,12},{5,13},{6,14},{7,15},{8,0},{9,1},... | collective-permute-start | bytes 786440 | tf_op jit(solution)/shard_map/ppermute | solution.py:13
  65.3 12.8 %collective-permute-start.14 = (bf16[256,2,256]{2,0,1:T(8,128)(2,1)}, bf16[256,2,256]{2,0,1:T(8,128)(2,1)}, u32[]{:S(2)}, u32[]{:S(2)}) collective-permute-start(bf16[256,2,256]{2,0,1:T(8,128)(2,1)} %fusion.40), channel_id=1, source_target_pairs={{0,4},{1,5},{2,6},{3,7},{4,0},{5,1},{6,2},{7,3},{8,12},{9,13},{10,... | collective-permute-start | bytes 786440 | tf_op jit(solution)/shard_map/ppermute | solution.py:13
  68.4 12.4 %collective-permute-start.13 = (bf16[256,2,256]{2,0,1:T(8,128)(2,1)}, bf16[256,2,256]{2,0,1:T(8,128)(2,1)}, u32[]{:S(2)}, u32[]{:S(2)}) collective-permute-start(bf16[256,2,256]{2,0,1:T(8,128)(2,1)} %fusion.39), channel_id=1, source_target_pairs={{0,2},{1,3},{2,0},{3,1},{4,6},{5,7},{6,4},{7,5},{8,10},{9,11},{10,... | collective-permute-start | bytes 786440 | tf_op jit(solution)/shard_map/ppermute | solution.py:13
  70.1 12.4 %collective-permute-start.12 = (bf16[256,2,256]{2,0,1:T(8,128)(2,1)S(1)}, bf16[256,2,256]{2,0,1:T(8,128)(2,1)}, u32[]{:S(2)}, u32[]{:S(2)}) collective-permute-start(bf16[256,2,256]{2,0,1:T(8,128)(2,1)S(1)} %fusion.38), channel_id=1, source_target_pairs={{0,1},{1,0},{2,3},{3,2},{4,5},{5,4},{6,7},{7,6},{8,9},{9,8},{10,11... | collective-permute-start | bytes 786440 | tf_op jit(solution)/shard_map/ppermute | solution.py:13
  73.4 49.6 %collective-permute-start.11 = (bf16[256,2,256]{2,0,1:T(8,128)(2,1)S(1)}, bf16[256,2,256]{2,0,1:T(8,128)(2,1)}, u32[]{:S(2)}, u32[]{:S(2)}) collective-permute-start(bf16[256,2,256]{2,0,1:T(8,128)(2,1)S(1)} %get-tuple-element.34), channel_id=1, source_target_pairs={{0,32},{1,33},{2,34},{3,35},{4,36},{5,37},{6,38},{7,39},{8,40},{9,... | collective-permute-start | bytes 786440 | tf_op jit(solution)/shard_map/ppermute | solution.py:13
  77.0 44.0 %collective-permute-start.10 = (bf16[256,2,256]{2,0,1:T(8,128)(2,1)S(1)}, bf16[256,2,256]{2,0,1:T(8,128)(2,1)}, u32[]{:S(2)}, u32[]{:S(2)}) collective-permute-start(bf16[256,2,256]{2,0,1:T(8,128)(2,1)S(1)} %get-tuple-element.34), channel_id=1, source_target_pairs={{0,16},{1,17},{2,18},{3,19},{4,20},{5,21},{6,22},{7,23},{8,24},{9,... | collective-permute-start | bytes 786440 | tf_op jit(solution)/shard_map/ppermute | solution.py:13
  78.1 41.0 %collective-permute-start.9 = (bf16[256,2,256]{2,0,1:T(8,128)(2,1)S(1)}, bf16[256,2,256]{2,0,1:T(8,128)(2,1)}, u32[]{:S(2)}, u32[]{:S(2)}) collective-permute-start(bf16[256,2,256]{2,0,1:T(8,128)(2,1)S(1)} %get-tuple-element.34), channel_id=1, source_target_pairs={{0,8},{1,9},{2,10},{3,11},{4,12},{5,13},{6,14},{7,15},{8,0},{9,1},... | collective-permute-start | bytes 786440 | tf_op jit(solution)/shard_map/ppermute | solution.py:13
  80.8 28.9 %collective-permute-start.7 = (bf16[256,2,256]{2,0,1:T(8,128)(2,1)S(1)}, bf16[256,2,256]{2,0,1:T(8,128)(2,1)}, u32[]{:S(2)}, u32[]{:S(2)}) collective-permute-start(bf16[256,2,256]{2,0,1:T(8,128)(2,1)S(1)} %get-tuple-element.34), channel_id=1, source_target_pairs={{0,2},{1,3},{2,0},{3,1},{4,6},{5,7},{6,4},{7,5},{8,10},{9,11},{10,... | collective-permute-start | bytes 786440 | tf_op jit(solution)/shard_map/ppermute | solution.py:13
  82.5 26.2 %collective-permute-start.6 = (bf16[256,2,256]{2,0,1:T(8,128)(2,1)S(1)}, bf16[256,2,256]{2,0,1:T(8,128)(2,1)S(1)}, u32[]{:S(2)}, u32[]{:S(2)}) collective-permute-start(bf16[256,2,256]{2,0,1:T(8,128)(2,1)S(1)} %get-tuple-element.34), channel_id=1, source_target_pairs={{0,1},{1,0},{2,3},{3,2},{4,5},{5,4},{6,7},{7,6},{8,9},{9,8},{10,11... | collective-permute-start | bytes 786440 | tf_op jit(solution)/shard_map/ppermute | solution.py:13
  108.7 12.4 %copy-start.4 = (bf16[256,2,256]{2,0,1:T(8,128)(2,1)}, bf16[256,2,256]{2,0,1:T(8,128)(2,1)S(1)}, u32[]{:S(2)}) copy-start(bf16[256,2,256]{2,0,1:T(8,128)(2,1)S(1)} %collective-permute-done.6) | copy-start | bytes 786436
  108.7 9.4 %collective-permute-start.8 = (bf16[256,2,256]{2,0,1:T(8,128)(2,1)S(1)}, bf16[256,2,256]{2,0,1:T(8,128)(2,1)S(1)}, u32[]{:S(2)}, u32[]{:S(2)}) collective-permute-start(bf16[256,2,256]{2,0,1:T(8,128)(2,1)S(1)} %get-tuple-element.34), channel_id=1, source_target_pairs={{0,4},{1,5},{2,6},{3,7},{4,0},{5,1},{6,2},{7,3},{8,12},{9,13},{10,... | collective-permute-start | bytes 786440 | tf_op jit(solution)/shard_map/ppermute | solution.py:13
  118.1 6.8 %copy-start.9 = (bf16[256,2,256]{2,0,1:T(8,128)(2,1)}, bf16[256,2,256]{2,0,1:T(8,128)(2,1)S(1)}, u32[]{:S(2)}) copy-start(bf16[256,2,256]{2,0,1:T(8,128)(2,1)S(1)} %collective-permute-done.8) | copy-start | bytes 786436
  132.8 46.1 %collective-permute-start.23 = (bf16[256,2,256]{0,2,1:T(8,128)(2,1)}, bf16[256,2,256]{0,2,1:T(8,128)(2,1)}, u32[]{:S(2)}, u32[]{:S(2)}) collective-permute-start(bf16[256,2,256]{0,2,1:T(8,128)(2,1)} %fusion.36), channel_id=1, source_target_pairs={{0,32},{1,33},{2,34},{3,35},{4,36},{5,37},{6,38},{7,39},{8,40},{9,... | collective-permute-start | bytes 786440 | tf_op jit(solution)/shard_map/ppermute | solution.py:13
  136.5 45.3 %collective-permute-start.22 = (bf16[256,2,256]{0,2,1:T(8,128)(2,1)}, bf16[256,2,256]{0,2,1:T(8,128)(2,1)}, u32[]{:S(2)}, u32[]{:S(2)}) collective-permute-start(bf16[256,2,256]{0,2,1:T(8,128)(2,1)} %fusion.35), channel_id=1, source_target_pairs={{0,16},{1,17},{2,18},{3,19},{4,20},{5,21},{6,22},{7,23},{8,24},{9,... | collective-permute-start | bytes 786440 | tf_op jit(solution)/shard_map/ppermute | solution.py:13
  137.5 44.4 %collective-permute-start.21 = (bf16[256,2,256]{0,2,1:T(8,128)(2,1)}, bf16[256,2,256]{0,2,1:T(8,128)(2,1)}, u32[]{:S(2)}, u32[]{:S(2)}) collective-permute-start(bf16[256,2,256]{0,2,1:T(8,128)(2,1)} %fusion.34), channel_id=1, source_target_pairs={{0,8},{1,9},{2,10},{3,11},{4,12},{5,13},{6,14},{7,15},{8,0},{9,1},... | collective-permute-start | bytes 786440 | tf_op jit(solution)/shard_map/ppermute | solution.py:13
  142.6 39.3 %collective-permute-start.20 = (bf16[256,2,256]{0,2,1:T(8,128)(2,1)}, bf16[256,2,256]{0,2,1:T(8,128)(2,1)}, u32[]{:S(2)}, u32[]{:S(2)}) collective-permute-start(bf16[256,2,256]{0,2,1:T(8,128)(2,1)} %fusion.33), channel_id=1, source_target_pairs={{0,4},{1,5},{2,6},{3,7},{4,0},{5,1},{6,2},{7,3},{8,12},{9,13},{10,... | collective-permute-start | bytes 786440 | tf_op jit(solution)/shard_map/ppermute | solution.py:13
  144.0 37.9 %collective-permute-start.19 = (bf16[256,2,256]{0,2,1:T(8,128)(2,1)}, bf16[256,2,256]{0,2,1:T(8,128)(2,1)}, u32[]{:S(2)}, u32[]{:S(2)}) collective-permute-start(bf16[256,2,256]{0,2,1:T(8,128)(2,1)} %fusion.32), channel_id=1, source_target_pairs={{0,2},{1,3},{2,0},{3,1},{4,6},{5,7},{6,4},{7,5},{8,10},{9,11},{10,... | collective-permute-start | bytes 786440 | tf_op jit(solution)/shard_map/ppermute | solution.py:13
  145.4 27.9 %copy-start.13 = (bf16[2,256,256]{2,1,0:T(8,128)(2,1)S(1)}, bf16[2,256,256]{2,1,0:T(8,128)(2,1)}, u32[]{:S(2)}) copy-start(bf16[2,256,256]{2,1,0:T(8,128)(2,1)} %param.14) | copy-start | bytes 786436
  178.9 3.0 collective-permute-start.18
  (11 other events, 38.1 us)
Sparse Core Ops, SparseCore 0:
  131.9 170.9 all-reduce.2
where the time goes:
time: 320 us; the launch traced here: 319 us
  waiting for transfers between devices  126 us (39%)
  matrix products  63.5 us (20%)
  starting transfers between devices  42.2 us (13%)
  between operations  28 us (9%)
  blocking collectives  26.2 us (8%)
  local copies, waits for them, and re-layouts  24 us (8%)
  other arithmetic  8.33 us (3%)
    psum x1, waiting for transfers between devices, on_device(): lax.psum(first_diag.astype(jnp.bfloat16), 'dp').astype(jnp.float32)  118 us
    ppermute x24, starting transfers between devices, from_partner(): return lax.ppermute(value, axis, pairs)  42.2 us
    psum x1, blocking collectives, on_device(): lax.psum(bias_partial.astype(jnp.bfloat16), 'dp').astype(jnp.float32)  26.2 us
    dot_general x14, matrix products, weight_partials(): jnp.einsum('tib,tic->ibc', other, grad, preferred_element_type=jnp.float32)  22.3 us
    dot_general x14, matrix products, backward_mix(): jnp.einsum('tic,ibc->tib', grad, weight, preferred_element_type=jnp.float32)  18.2 us
    dot_general x14, matrix products, forward_mix(): jnp.einsum('tib,ibc->tic', other, weight, preferred_element_type=jnp.floa...  15.2 us
    unnamed x44, local copies, waits for them, and re-layouts  12.6 us
    ppermute x24, waiting for transfers between devices, from_partner(): return lax.ppermute(value, axis, pairs)  7.98 us
  transfers between devices with their start and end apart: 25, of which 6 were waited for; matrix products, arithmetic and copies ran while one was open for 24% of the time, Pallas kernels for 0%

commit v1 on v0

v1 whole, which is shorter than its diff:
```python
import jax
import jax.numpy as jnp
from jax import lax
from jax.experimental import pallas as pl
from jax.experimental.pallas import tpu as pltpu
from jax.sharding import PartitionSpec as P

SECTIONS = 7
BS = 256
COLS = 512
ROWS = 256
REST = 768
N_DP = 4
N_FEAT = 64
CORE, X1, X2, ZHI, Y1, Y2 = range(6)
DEVICE_BITS = 6
FEAT = ("y", "z_hi", "x_core")
NEAR = (CORE, X1, X2, Y1, Y2)
START_ORDER = (ZHI, X2, Y2, CORE, X1, Y1)
SQRT_2_OVER_PI = 0.7978845608028654
CUBIC = 0.044715
VMEM_LIMIT = 60 * 1024 * 1024
BF16 = jnp.bfloat16
F32 = jnp.float32


def after(*values):
    return lax.optimization_barrier(values)


def from_partner(value, bit):
    pairs = [(source, source ^ (1 << bit)) for source in range(N_FEAT)]
    return lax.ppermute(value, FEAT, pairs)


def send(values):
    return {bit: from_partner(value, bit) for bit, value in values.items()}


def join(arrived, *values):
    tied = after(*arrived.values(), *values)
    return dict(zip(arrived, tied)), tied[len(arrived) :]


def tie(pair, *values):
    tied = after(*pair, *values)
    return tied[:2], tied[2:]


def along_z(value, step):
    pairs = []
    for dp in range(N_DP):
        for feat in range(N_FEAT):
            z_hi = (feat >> 3) & 1
            z = (z_hi * N_DP + dp + step) % (2 * N_DP)
            to_feat = (feat & ~8) | ((z // N_DP) << 3)
            pairs.append((dp * N_FEAT + feat, (z % N_DP) * N_FEAT + to_feat))
    return lax.ppermute(value, ("dp", *FEAT), pairs)


def both_ways(up, down):
    return along_z(up, 1), along_z(down, -1)


LINE = (
    ((1, 0), (1, 1), (1, 2)),
    ((1, 0), (1, 1), (0, 0)),
    ((1, 0), (0, 1), (0, 0)),
    ((0, 0), (0, 1), (0, 2)),
)
FAR = (
    ((0, 2), (0, 1), (0, 0)),
    ((0, 2), (0, 1), (1, 2)),
    ((0, 2), (1, 1), (1, 2)),
    ((1, 2), (1, 1), (1, 0)),
)


def dot(a, b):
    return jnp.dot(a, b, preferred_element_type=F32)


def dot_t(a, b):
    return lax.dot_general(a, b, (((1,), (1,)), ((), ())), preferred_element_type=F32)


def t_dot(a, b):
    return lax.dot_general(a, b, (((0,), (0,)), ((), ())), preferred_element_type=F32)


def sections_of(bits):
    return [
        sum(jnp.where(bits[section] == level, section, 0) for section in range(SECTIONS))
        for level in range(SECTIONS)
    ]


def half(block):
    return slice(block * BS, (block + 1) * BS)


def mix_block(order, own, others, diag, part, block):
    total = dot(own[0:ROWS, half(block)], diag[block])
    total = total + dot(own[0:ROWS, half(1 - block)], part[order[0], block])
    for bit in range(DEVICE_BITS):
        total = total + dot(others[bit][0:ROWS, half(block)], part[order[bit + 1], block])
    return total


def products(order, grad, diag, part, local, sent):
    for block in range(2):
        value = grad[:, half(block)]
        other = grad[:, half(1 - block)]
        local[:, half(block)] = dot_t(value, diag[block]) + dot_t(other, part[order[0], 1 - block])
        for bit in range(DEVICE_BITS):
            term = dot_t(value, part[order[bit + 1], block]).astype(BF16)
            sent[bit][sent[bit].shape[0] - ROWS :, half(block)] = term


def first_kernel(bits, features, grad, diag, part, local, *sent):
    order = sections_of(bits)
    for bit in range(DEVICE_BITS):
        sent[bit][0:ROWS] = features[...]
    products(order, grad, diag, part, local, sent)


def middle_kernel(bits, features, local_in, *refs):
    got, (diag, part, bias, late, local, *sent) = refs[:6], refs[6:]
    order = sections_of(bits)
    for block in range(2):
        pre = mix_block(order, features, got, diag, part, block)
        pre = pre + bias[half(block)].astype(F32)[None, :]
        tanh = jnp.tanh(SQRT_2_OVER_PI * (pre + CUBIC * pre * pre * pre))
        hidden = (0.5 * pre * (1.0 + tanh)).astype(BF16)
        late[0:ROWS, half(block)] = hidden
        for bit in NEAR:
            sent[bit][0:ROWS, half(block)] = hidden
        total = local_in[:, half(block)]
        for bit in range(DEVICE_BITS):
            total = total + got[bit][ROWS:, half(block)].astype(F32)
        slope = SQRT_2_OVER_PI * (1.0 + (3.0 * CUBIC) * pre * pre)
        gain = 0.5 * (1.0 + tanh) + 0.5 * pre * (1.0 - tanh * tanh) * slope
        late[ROWS : 2 * ROWS, half(block)] = (total * gain).astype(BF16)
    products(order, late.at[ROWS : 2 * ROWS], diag, part, local, sent)


def last_kernel(bits, hidden, *refs):
    order = sections_of(bits)
    got, got_far, far, (local, diag, part, out, grad_in) = refs[:5], refs[5], refs[6], refs[7:]
    others = dict(zip(NEAR, got))
    others[ZHI] = far
    for block in range(2):
        total = mix_block(order, hidden, others, diag, part, block)
        out[:, half(block)] = total.astype(BF16)
    total = local[...] + got_far[...].astype(F32)
    for ref in got:
        total = total + ref[ROWS:].astype(F32)
    grad_in[...] = total.astype(BF16)


def of_this_dp(body):
    for dp in range(N_DP):

        @pl.when(lax.axis_index("dp") == dp)
        def _():
            body(dp)


def rows_kernel(bits, *refs):
    chunks, out, sem = (refs[0:3], refs[3:6]), refs[6], refs[7]

    def copy(way, step, at):
        return pltpu.make_async_copy(
            chunks[way][step].at[pl.ds(0, ROWS)], out.at[pl.ds(at * ROWS, ROWS)], sem.at[at]
        )

    @of_this_dp
    def _(dp):
        for at, (way, step) in enumerate(LINE[dp]):
            copy(way, step, at).start()

    for at in range(3):
        copy(0, 0, at).wait()


def other_dp(dp, at):
    way, step = LINE[dp][at]
    return dp + 1 + step if way else dp - 1 - step


def gathered_row(dp, far, rows):
    z_hi = lax.axis_index("z_hi")
    if far:
        z_hi = 1 - z_hi
    return pl.multiple_of((z_hi * N_DP + dp) * rows, rows)


def hidden_rows_kernel(bits, gathered, rows, far, sem):
    def copy(row, out, at, order):
        return pltpu.make_async_copy(
            gathered.at[pl.ds(row, ROWS)], out.at[pl.ds(at * ROWS, ROWS)], sem.at[order]
        )

    @of_this_dp
    def _(dp):
        for at in range(3):
            copy(gathered_row(other_dp(dp, at), False, 2 * ROWS), rows, at, at).start()
        copy(gathered_row(dp, True, 2 * ROWS), far, 0, 3).start()

    for at in range(3):
        copy(0, rows, at, at).wait()
    copy(0, far, 0, 3).wait()


def weight_kernel(second, bits, *refs):
    order = sections_of(bits)
    own, own_rest, far, grad, gathered = refs[0:5]
    near, near_rest = refs[5:10], refs[10:15]
    chunks = (refs[15:18], refs[18:21])
    diag_out, part_out, bias_out, own_buf, far_buf, grad_buf, near_buf, sems = refs[21:]

    def copy(source, at, rows, target, to, sem):
        return pltpu.make_async_copy(
            source.at[pl.ds(at, rows)], target.at[pl.ds(to, rows)], sems.at[sem]
        )

    def grad_copy(at, source, row):
        return copy(source, row, ROWS, grad_buf, (at + 1) * ROWS, 1 + at)

    def far_copy(at, source, row):
        return copy(source, row, ROWS, far_buf, (at + 1) * ROWS, 7 + at)

    grad_copies = [copy(grad, 0 if second else ROWS, ROWS, grad_buf, 0, 0)]
    grad_copies += [grad_copy(at, gathered, 0) for at in range(3)]
    far_copies = [copy(far, 0, ROWS, far_buf, 0, 6)]
    far_copies += [far_copy(at, gathered, 0) for at in range(3)]
    own_copies = [
        copy(own, 0, ROWS, own_buf, 0, 4),
        copy(own_rest, 0, REST, own_buf, ROWS, 5),
    ]
    near_copies = []
    for at in range(5):
        buf = near_buf.at[at]
        near_copies.append(
            [
                copy(near[at], 0, ROWS, buf, 0, 10 + 2 * at),
                copy(near_rest[at], 0, REST, buf, ROWS, 11 + 2 * at),
            ]
        )
    grad_copies[0].start()

    @of_this_dp
    def _(dp):
        for at in range(3):
            other = other_dp(dp, at)
            if second:
                way, step = LINE[dp][at]
                source = chunks[way][step]
                grad_copy(at, source, source.shape[0] - ROWS).start()
                far_copy(at, gathered, gathered_row(other, True, 2 * ROWS)).start()
            else:
                row = gathered_row(other, False, 2 * ROWS)
                grad_copy(at, gathered, row + ROWS).start()
                way, step = FAR[dp][at]
                far_copy(at, chunks[way][step], 0).start()

    for item in (*own_copies, far_copies[0]):
        item.start()
    for pair in near_copies:
        for item in pair:
            item.start()
    for item in grad_copies:
        item.wait()
    for block in range(2):
        total = jnp.sum(grad_buf[:, half(block)].astype(F32), axis=0, keepdims=True)
        bias_out[half(block)] = total[0].astype(BF16)
    for item in own_copies:
        item.wait()
    for block in range(2):
        grads = grad_buf[:, half(block)]
        diag_out[block] = t_dot(own_buf[:, half(block)], grads).astype(BF16)
        part_out[order[0], block] = t_dot(own_buf[:, half(1 - block)], grads).astype(BF16)
    for item in far_copies:
        item.wait()
    for block in range(2):
        term = t_dot(far_buf[:, half(block)], grad_buf[:, half(block)])
        part_out[order[ZHI + 1], block] = term.astype(BF16)
    for at, bit in enumerate(NEAR):
        for item in near_copies[at]:
            item.wait()
        for block in range(2):
            term = t_dot(near_buf[at, :, half(block)], grad_buf[:, half(block)])
            part_out[order[bit + 1], block] = term.astype(BF16)


def shape(rows, dtype=BF16):
    return jax.ShapeDtypeStruct((rows, COLS), dtype)


def whole(value):
    zeros = (0,) * len(value.shape)
    return pl.BlockSpec(value.shape, lambda step: zeros)


HBM = pl.BlockSpec(memory_space=pl.ANY)
SCALARS = pl.BlockSpec(memory_space=pltpu.SMEM)
MAP_FLOPS = 2 * 16 * BS * BS * BS


def call(kernel, name, out_shape, flops, bits, args, fetch=True, scratch=(), outs=None):
    moved = sum(a.size * a.dtype.itemsize for a in (*args, *out_shape))
    return pl.pallas_call(
        kernel,
        grid=(1,),
        out_shape=out_shape,
        in_specs=[SCALARS] + [whole(value) if fetch else HBM for value in args],
        out_specs=outs or [whole(value) for value in out_shape],
        scratch_shapes=scratch,
        compiler_params=pltpu.CompilerParams(vmem_limit_bytes=VMEM_LIMIT),
        cost_estimate=pl.CostEstimate(flops=flops, bytes_accessed=moved, transcendentals=0),
        name=name,
    )(bits, *args)


def chunks_of(steps):
    return [item[0] for item in steps] + [item[1] for item in steps]


def rows_of_line(name, bits, steps):
    (rows,) = call(
        rows_kernel,
        name,
        (shape(REST),),
        0,
        bits,
        chunks_of(steps),
        fetch=False,
        scratch=[pltpu.SemaphoreType.DMA((3,))],
    )
    return rows


def weight_sums(name, bits, second, args):
    def kernel(*refs):
        weight_kernel(second, *refs)

    stacked = (N_DP * ROWS, COLS)
    return call(
        kernel,
        name,
        (
            jax.ShapeDtypeStruct((2, BS, BS), BF16),
            jax.ShapeDtypeStruct((SECTIONS, 2, BS, BS), BF16),
            jax.ShapeDtypeStruct((COLS,), BF16),
        ),
        N_DP * MAP_FLOPS,
        bits,
        args,
        fetch=False,
        scratch=[
            pltpu.VMEM(stacked, BF16),
            pltpu.VMEM(stacked, BF16),
            pltpu.VMEM(stacked, BF16),
            pltpu.VMEM((5, *stacked), BF16),
            pltpu.SemaphoreType.DMA((20,)),
        ],
    )


def on_device(
    features, diag_first, part_first, bias_first, diag_second, part_second, section_bit, grad_out
):
    bits = range(DEVICE_BITS)

    features_z = [both_ways(features, features)]
    local_second, *sent = call(
        first_kernel,
        "products_second",
        (shape(ROWS, F32), *[shape(2 * ROWS)] * 6),
        MAP_FLOPS,
        section_bit,
        (features, grad_out, diag_second, part_second),
    )
    *ends, local_second = after(*features_z[0], *sent, local_second)
    sent = ends[2:]
    got = send({bit: sent[bit] for bit in START_ORDER})
    up, down, *tied = after(*ends[:2], *[got[bit] for bit in bits])
    got = dict(zip(bits, tied))
    features_z[0] = (up, down)
    features_z.append(
        both_ways(*[jnp.concatenate([value, grad_out], axis=0) for value in (up, down)])
    )
    late, local_first, *sent = call(
        middle_kernel,
        "hidden_and_grad_pre",
        (shape(2 * ROWS), shape(ROWS, F32))
        + tuple(shape(ROWS if bit == ZHI else 2 * ROWS) for bit in bits),
        2 * MAP_FLOPS,
        section_bit,
        (
            features,
            local_second,
            *[got[bit] for bit in bits],
            diag_first,
            part_first,
            bias_first,
        ),
    )
    up, down, late = after(*features_z[1], late)
    features_z[1] = (up, down)
    gathered = lax.all_gather(late, ("z_hi", "dp"), axis=0, tiled=True)
    features_z.append(both_ways(up, down))
    got_late = send({bit: sent[bit] for bit in (X2, Y2, X1)})
    features_z[2], (sent[Y1], sent[CORE]) = tie(features_z[2], sent[Y1], sent[CORE])
    got_late.update(send({Y1: sent[Y1], CORE: sent[CORE]}))
    feature_rows = rows_of_line("feature_rows", section_bit, features_z)
    feature_rows, got_late[X2], got_late[Y2] = after(feature_rows, got_late[X2], got_late[Y2])
    feature_near = send({X2: feature_rows, Y2: feature_rows})
    got_late, (feature_rows,) = join(got_late, feature_rows)
    feature_near.update(send({X1: feature_rows, Y1: feature_rows, CORE: feature_rows}))
    gathered, feature_near[X2], feature_near[Y2] = after(
        gathered, feature_near[X2], feature_near[Y2]
    )
    hidden_rows, hidden_far = call(
        hidden_rows_kernel,
        "hidden_rows",
        (shape(REST), shape(ROWS)),
        0,
        section_bit,
        (gathered,),
        fetch=False,
        scratch=[pltpu.SemaphoreType.DMA((4,))],
    )
    hidden_near = send({X2: hidden_rows, Y2: hidden_rows})
    feature_near, (hidden_rows,) = join(feature_near, hidden_rows)
    hidden_near.update(send({X1: hidden_rows, Y1: hidden_rows, CORE: hidden_rows}))
    far_product, hidden_near[CORE] = after(sent[ZHI], hidden_near[CORE])
    got_late[ZHI] = from_partner(far_product, ZHI)
    up, down, hidden_near[X2], hidden_near[Y2] = after(
        *features_z[2], hidden_near[X2], hidden_near[Y2]
    )
    grad_z = [*features_z[1:], both_ways(up[ROWS:], down[ROWS:])]
    diag_first_grad, part_first_grad, bias_grad = weight_sums(
        "weights_first",
        section_bit,
        False,
        (
            features,
            feature_rows,
            got[ZHI],
            late,
            gathered,
            *[got[bit] for bit in NEAR],
            *[feature_near[bit] for bit in NEAR],
            *chunks_of(features_z),
        ),
    )
    output, grad_in = call(
        last_kernel,
        "output_and_grad_features",
        (shape(ROWS), shape(ROWS)),
        MAP_FLOPS,
        section_bit,
        (
            late,
            *[got_late[bit] for bit in NEAR],
            got_late[ZHI],
            hidden_far,
            local_first,
            diag_second,
            part_second,
        ),
    )
    hidden_near = after(*[hidden_near[bit] for bit in NEAR], bias_grad, output)[:5]
    diag_second_grad, part_second_grad, _ = weight_sums(
        "weights_second",
        section_bit,
        True,
        (
            late,
            hidden_rows,
            hidden_far,
            grad_out,
            gathered,
            *[got_late[bit] for bit in NEAR],
            *hidden_near,
            *chunks_of(grad_z),
        ),
    )
    return (
        output,
        grad_in,
        diag_first_grad,
        part_first_grad,
        bias_grad,
        diag_second_grad,
        part_second_grad,
    )


def solution(mesh):
    mesh = jax.sharding.Mesh(mesh.devices.reshape(N_DP, 4, 2, 8), ("dp", *FEAT))
    in_specs = (
        P("dp", FEAT),
        P(FEAT, None, None),
        P(None, FEAT, None, None),
        P(FEAT),
        P(FEAT, None, None),
        P(None, FEAT, None, None),
        P(),
        P("dp", FEAT),
    )
    out_specs = (
        P("dp", FEAT),
        P("dp", FEAT),
        P(FEAT, None, None),
        P(None, FEAT, None, None),
        P(FEAT),
        P(FEAT, None, None),
        P(None, FEAT, None, None),
    )
    return jax.shard_map(
        on_device, mesh=mesh, in_specs=in_specs, out_specs=out_specs, check_vma=False
    )
```

time: 320 us -> 197 us (0.62)
  matrix products: 63.5 us -> 0 us
  Pallas kernels: 0 us -> 35.9 us
  waiting for transfers between devices: 126 us -> 90.7 us
  blocking collectives: 26.2 us -> 0 us
  local copies, waits for them, and re-layouts: 24 us -> 2.43 us
  between operations: 28 us -> 14.3 us
  starting transfers between devices: 42.2 us -> 51.9 us
  other arithmetic: 8.33 us -> 1.14 us
    psum x1 -> x0, waiting for transfers between devices: 118 us -> none  [on_device(): lax.psum(first_diag.astype(jnp.bfloat16), 'dp').astype(jnp.float32)]
    ppermute x24 -> x30, waiting for transfers between devices: 7.98 us -> 89.2 us  [the longest x22 69.9 us: from_partner(): return lax.ppermute(value, FEAT, pairs)]
    dot_general x48 -> x0, matrix products: 63.5 us -> none  [the longest x14 22.3 us: weight_partials(): jnp.einsum('tib,tic->ibc', other, grad, preferred_element_type=jnp.float32)]
    pallas_call x0 -> x7, Pallas kernels: none -> 35.9 us  [call(): pl.pallas_call(kernel, grid=(1,), out_shape=out_shape, in_specs=[SCALARS]...]
    psum x1 -> x0, blocking collectives: 26.2 us -> none  [on_device(): lax.psum(bias_partial.astype(jnp.bfloat16), 'dp').astype(jnp.float32)]
    unnamed x44 -> x46, local copies, waits for them, and re-layouts: 12.6 us -> 1.65 us
    ppermute x24 -> x30, starting transfers between devices: 42.2 us -> 51.8 us  [the longest x22 37.6 us: from_partner(): return lax.ppermute(value, FEAT, pairs)]
    convert_element_type x2 -> x0, other arithmetic: 6.88 us -> none  [the longest x1 3.44 us: on_device(): first_part.astype(jnp.bfloat16)]
  transfers between devices with their start and end apart: 25 -> 31, of which waited for: 6 -> 15; matrix products, arithmetic and copies ran while one was open for 24% -> 0% of each run, Pallas kernels for 0% -> 14%
where the time goes in v1:
time: 197 us; the launch traced here: 196 us
  waiting for transfers between devices  90.7 us (46%)
  starting transfers between devices  51.9 us (26%)
  Pallas kernels  35.9 us (18%)
  between operations  14.3 us (7%)
  local copies, waits for them, and re-layouts  2.43 us (1%)
    ppermute x22, waiting for transfers between devices, from_partner(): return lax.ppermute(value, FEAT, pairs)  69.9 us
    ppermute x22, starting transfers between devices, from_partner(): return lax.ppermute(value, FEAT, pairs)  37.6 us
    pallas_call x7, Pallas kernels, call(): pl.pallas_call(kernel, grid=(1,), out_shape=out_shape, in_specs=[SCALARS]...  35.9 us
    ppermute x8, waiting for transfers between devices, along_z(): return lax.ppermute(value, ('dp', *FEAT), pairs)  19.3 us
    ppermute x8, starting transfers between devices, along_z(): return lax.ppermute(value, ('dp', *FEAT), pairs)  14.2 us
  transfers between devices with their start and end apart: 31, of which 15 were waited for; matrix products, arithmetic and copies ran while one was open for 0% of the time, Pallas kernels for 14%

profile of v1, /device:TPU:1, one launch (start us, length us, event | category | flops | bytes accessed | tf_op | source)
XLA Modules:
  0.0 196.3 jit_solution(11879325990821672477)
XLA Ops:
  7.2 6.5 %collective-permute-start.1 = (bf16[256,512]{1,0:T(8,128)(2,1)}, bf16[256,512]{1,0:T(8,128)(2,1)S(1)}, u32[]{:S(2)}, u32[]{:S(2)}) collective-permute-start(bf16[256,512]{1,0:T(8,128)(2,1)} %refs_1_.1), channel_id=1, source_target_pairs={{0,200},{1,201},{2,202},{3,203},{4,204},{5,205},{6,206},{7,207},{8... | collective-permute-start | bytes 786440 | tf_op jit(solution)/shard_map/ppermute | solution.py:58
  13.7 4.2 %products_second.1 = (f32[256,512]{1,0:T(8,128)}, bf16[512,512]{1,0:T(8,128)(2,1)}, bf16[512,512]{1,0:T(8,128)(2,1)}, bf16[512,512]{1,0:T(8,128)(2,1)}, bf16[512...) custom-call(s32[7]{0:T(128)} %refs_0_.3, bf16[256,512]{1,0:T(8,128)(2,1)} %refs_1_.1, ...), custom_call_target="tpu_custom_call" | custom-call | flops 536870912 | bytes 6291456 | tf_op jit(solution)/shard_map/products_second/pallas_call | solution.py:312
  19.0 3.0 %collective-permute-done.refs_0_.refs_16_ = bf16[256,512]{1,0:T(8,128)(2,1)S(1)} collective-permute-done((bf16[256,512]{1,0:T(8,128)(2,1)}, bf16[256,512]{1,0:T(8,128)(2,1)S(1)}, u32[]{:S(2)}, u32[]{:S(2)}) %collective-permute-start) | collective-permute-done | bytes 262176 | tf_op jit(solution)/shard_map/ppermute | solution.py:58
  22.0 1.9 collective-permute-start.2
  25.1 2.5 %collective-permute-start.4 = (bf16[512,512]{1,0:T(8,128)(2,1)}, bf16[512,512]{1,0:T(8,128)(2,1)S(1)}, u32[]{:S(2)}, u32[]{:S(2)}) collective-permute-start(bf16[512,512]{1,0:T(8,128)(2,1)} %get-tuple-element.95), channel_id=1, source_target_pairs={{0,4},{1,5},{2,6},{3,7},{4,0},{5,1},{6,2},{7,3},{8,12},{9,13},{10,... | collective-permute-start | bytes 1572872 | tf_op jit(solution)/shard_map/ppermute | solution.py:33
  30.2 2.6 %collective-permute-start.7 = (bf16[512,512]{1,0:T(8,128)(2,1)}, bf16[512,512]{1,0:T(8,128)(2,1)S(1)}, u32[]{:S(2)}, u32[]{:S(2)}) collective-permute-start(bf16[512,512]{1,0:T(8,128)(2,1)} %get-tuple-element.98), channel_id=1, source_target_pairs={{0,32},{1,33},{2,34},{3,35},{4,36},{5,37},{6,38},{7,39},{8,40},{9,... | collective-permute-start | bytes 1572872 | tf_op jit(solution)/shard_map/ppermute | solution.py:33
  32.9 4.8 %collective-permute-done.3.refs_1_.refs_7_ = bf16[512,512]{1,0:T(8,128)(2,1)S(1)} collective-permute-done((bf16[512,512]{1,0:T(8,128)(2,1)}, bf16[512,512]{1,0:T(8,128)(2,1)S(1)}, u32[]{:S(2)}, u32[]{:S(2)}) %collective-permute-start.3) | collective-permute-done | bytes 524320 | tf_op jit(solution)/shard_map/ppermute | solution.py:33
  37.6 13.4 %collective-permute-done.4.refs_2_.refs_8_ = bf16[512,512]{1,0:T(8,128)(2,1)S(1)} collective-permute-done((bf16[512,512]{1,0:T(8,128)(2,1)}, bf16[512,512]{1,0:T(8,128)(2,1)S(1)}, u32[]{:S(2)}, u32[]{:S(2)}) %collective-permute-start.4) | collective-permute-done | bytes 524320 | tf_op jit(solution)/shard_map/ppermute | solution.py:33
  51.0 5.2 %collective-permute-done.5.refs_3_ = bf16[512,512]{1,0:T(8,128)(2,1)S(1)} collective-permute-done((bf16[512,512]{1,0:T(8,128)(2,1)}, bf16[512,512]{1,0:T(8,128)(2,1)S(1)}, u32[]{:S(2)}, u32[]{:S(2)}) %collective-permute-start.5) | collective-permute-done | bytes 524320 | tf_op jit(solution)/shard_map/ppermute | solution.py:33
  59.0 6.3 %hidden_and_grad_pre.1 = (bf16[512,512]{1,0:T(8,128)(2,1)}, f32[256,512]{1,0:T(8,128)}, bf16[512,512]{1,0:T(8,128)(2,1)}, bf16[512,512]{1,0:T(8,128)(2,1)}, bf16...) custom-call(s32[7]{0:T(128)} %refs_0_.3, ...), custom_call_target="tpu_custom_call" | custom-call | flops 1073741824 | bytes 9962496 | tf_op jit(solution)/shard_map/hidden_and_grad_pre/pallas_call | solution.py:312
  65.4 5.1 %collective-permute-done.9.refs_4_.refs_20_.refs_19_ = bf16[512,512]{1,0:T(8,128)(2,1)S(1)} collective-permute-done((bf16[512,512]{1,0:T(8,128)(2,1)}, bf16[512,512]{1,0:T(8,128)(2,1)S(1)}, u32[]{:S(2)}, u32[]{:S(2)}) %collective-permute-start.9) | collective-permute-done | bytes 524320 | tf_op jit(solution)/shard_map/ppermute | solution.py:58
  71.7 2.4 %collective-permute-start.11 = (bf16[512,512]{1,0:T(8,128)(2,1)S(1)}, bf16[512,512]{1,0:T(8,128)(2,1)S(1)}, u32[]{:S(2)}, u32[]{:S(2)}) collective-permute-start(bf16[512,512]{1,0:T(8,128)(2,1)S(1)} %collective-permute-done.9.refs_4_.refs_20_.refs_19_), channel_id=1, source_target_pairs={{0,200},{1,201},{2,202},{3,203},{4,204},{5,205},{6,206},{7,207},{8... | collective-permute-start | bytes 1572872 | tf_op jit(solution)/shard_map/ppermute | solution.py:58
  74.6 3.5 %collective-permute-start.13 = (bf16[512,512]{1,0:T(8,128)(2,1)}, bf16[512,512]{1,0:T(8,128)(2,1)S(1)}, u32[]{:S(2)}, u32[]{:S(2)}) collective-permute-start(bf16[512,512]{1,0:T(8,128)(2,1)} %get-tuple-element.117), channel_id=1, source_target_pairs={{0,32},{1,33},{2,34},{3,35},{4,36},{5,37},{6,38},{7,39},{8,40},{9,... | collective-permute-start | bytes 1572872 | tf_op jit(solution)/shard_map/ppermute | solution.py:33
  78.4 7.5 %collective-permute-done.10.refs_2_.refs_18_.refs_17_ = bf16[512,512]{1,0:T(8,128)(2,1)S(1)} collective-permute-done((bf16[512,512]{1,0:T(8,128)(2,1)S(1)}, bf16[512,512]{1,0:T(8,128)(2,1)S(1)}, u32[]{:S(2)}, u32[]{:S(2)}) %collective-permute-start.10) | collective-permute-done | bytes 524320 | tf_op jit(solution)/shard_map/ppermute | solution.py:58
  85.9 1.8 collective-permute-done.11.refs_5_.refs_21_.refs_20_
  87.7 3.9 %collective-permute-start.15 = (bf16[512,512]{1,0:T(8,128)(2,1)}, bf16[512,512]{1,0:T(8,128)(2,1)}, u32[]{:S(2)}, u32[]{:S(2)}) collective-permute-start(bf16[512,512]{1,0:T(8,128)(2,1)} %get-tuple-element.121), channel_id=1, source_target_pairs={{0,16},{1,17},{2,18},{3,19},{4,20},{5,21},{6,22},{7,23},{8,24},{9,... | collective-permute-start | bytes 1572872 | tf_op jit(solution)/shard_map/ppermute | solution.py:33
  91.6 7.1 %collective-permute-start.16 = (bf16[512,512]{1,0:T(8,128)(2,1)}, bf16[512,512]{1,0:T(8,128)(2,1)}, u32[]{:S(2)}, u32[]{:S(2)}) collective-permute-start(bf16[512,512]{1,0:T(8,128)(2,1)} %get-tuple-element.122), channel_id=1, source_target_pairs={{0,1},{1,0},{2,3},{3,2},{4,5},{5,4},{6,7},{7,6},{8,9},{9,8},{10,11... | collective-permute-start | bytes 1572872 | tf_op jit(solution)/shard_map/ppermute | solution.py:33
  98.7 2.7 %feature_rows.1.refs_2_ = bf16[768,512]{1,0:T(8,128)(2,1)} custom-call(s32[7]{0:T(128)} %refs_0_.3, bf16[256,512]{1,0:T(8,128)(2,1)} %copy-done.7, bf16[512,512]{1,0:T(8,128)(2,1)} %copy-done.5, bf16[512,512]{1,0:T(8,128)(2,1)} %copy-done, bf16[256,512]{1,0:T(8,128)(2,1)} %copy-done.6, bf16[512,512]{1,0:T(8,128)(2,1)} %copy-done.4, bf16[512,512]{1,0:T(8,128)(2,1)} %copy-done.2), custom_call_target="tpu_custom_call" | custom-call | bytes 3407872 | tf_op jit(solution)/shard_map/feature_rows/pallas_call | solution.py:312
  101.5 2.9 %collective-permute-start.18 = (bf16[768,512]{1,0:T(8,128)(2,1)}, bf16[768,512]{1,0:T(8,128)(2,1)S(1)}, u32[]{:S(2)}, u32[]{:S(2)}) collective-permute-start(bf16[768,512]{1,0:T(8,128)(2,1)} %feature_rows.1.refs_2_), channel_id=1, source_target_pairs={{0,32},{1,33},{2,34},{3,35},{4,36},{5,37},{6,38},{7,39},{8,40},{9,... | collective-permute-start | bytes 2359304 | tf_op jit(solution)/shard_map/ppermute | solution.py:33
  104.4 1.7 collective-permute-start.21
  106.2 1.8 collective-permute-start.20
  107.9 15.1 %collective-permute-done.18.refs_15_ = bf16[768,512]{1,0:T(8,128)(2,1)S(1)} collective-permute-done((bf16[768,512]{1,0:T(8,128)(2,1)}, bf16[768,512]{1,0:T(8,128)(2,1)S(1)}, u32[]{:S(2)}, u32[]{:S(2)}) %collective-permute-start.18) | collective-permute-done | bytes 786464 | tf_op jit(solution)/shard_map/ppermute | solution.py:33
  123.0 2.1 %collective-permute-done.17.refs_13_ = bf16[768,512]{1,0:T(8,128)(2,1)} collective-permute-done((bf16[768,512]{1,0:T(8,128)(2,1)}, bf16[768,512]{1,0:T(8,128)(2,1)}, u32[]{:S(2)}, u32[]{:S(2)}) %collective-permute-start.17) | collective-permute-done | bytes 786464 | tf_op jit(solution)/shard_map/ppermute | solution.py:33
  126.5 2.9 %hidden_rows.1 = (bf16[768,512]{1,0:T(8,128)(2,1)}, bf16[256,512]{1,0:T(8,128)(2,1)}) custom-call(s32[7]{0:T(128)} %refs_0_.3, bf16[4096,512]{1,0:T(8,128)(2,1)} %all-gather.2.cloned.1.call-done.gathered.refs_5_), custom_call_target="tpu_custom_call" | custom-call | bytes 5242880 | tf_op jit(solution)/shard_map/hidden_rows/pallas_call | solution.py:312
  129.4 9.5 %collective-permute-done.20.refs_14_ = bf16[768,512]{1,0:T(8,128)(2,1)} collective-permute-done((bf16[768,512]{1,0:T(8,128)(2,1)}, bf16[768,512]{1,0:T(8,128)(2,1)}, u32[]{:S(2)}, u32[]{:S(2)}) %collective-permute-start.20) | collective-permute-done | bytes 786464 | tf_op jit(solution)/shard_map/ppermute | solution.py:33
  139.9 3.5 %collective-permute-start.26 = (bf16[768,512]{1,0:T(8,128)(2,1)}, bf16[768,512]{1,0:T(8,128)(2,1)S(1)}, u32[]{:S(2)}, u32[]{:S(2)}) collective-permute-start(bf16[768,512]{1,0:T(8,128)(2,1)} %get-tuple-element.135.refs_2_), channel_id=1, source_target_pairs={{0,32},{1,33},{2,34},{3,35},{4,36},{5,37},{6,38},{7,39},{8,40},{9,... | collective-permute-start | bytes 2359304 | tf_op jit(solution)/shard_map/ppermute | solution.py:33
  144.0 17.4 %collective-permute-done.26.refs_15_ = bf16[768,512]{1,0:T(8,128)(2,1)S(1)} collective-permute-done((bf16[768,512]{1,0:T(8,128)(2,1)}, bf16[768,512]{1,0:T(8,128)(2,1)S(1)}, u32[]{:S(2)}, u32[]{:S(2)}) %collective-permute-start.26) | collective-permute-done | bytes 786464 | tf_op jit(solution)/shard_map/ppermute | solution.py:33
  161.5 2.4 %collective-permute-done.25.refs_13_ = bf16[768,512]{1,0:T(8,128)(2,1)S(1)} collective-permute-done((bf16[768,512]{1,0:T(8,128)(2,1)}, bf16[768,512]{1,0:T(8,128)(2,1)S(1)}, u32[]{:S(2)}, u32[]{:S(2)}) %collective-permute-start.25) | collective-permute-done | bytes 786464 | tf_op jit(solution)/shard_map/ppermute | solution.py:33
  164.7 3.5 %collective-permute-start.29 = (bf16[256,512]{1,0:T(8,128)(2,1)S(1)}, bf16[256,512]{1,0:T(8,128)(2,1)S(1)}, u32[]{:S(2)}, u32[]{:S(2)}) collective-permute-start(bf16[256,512]{1,0:T(8,128)(2,1)S(1)} %slice.7), channel_id=1, source_target_pairs={{0,200},{1,201},{2,202},{3,203},{4,204},{5,205},{6,206},{7,207},{8... | collective-permute-start | bytes 786440 | tf_op jit(solution)/shard_map/ppermute | solution.py:58
  168.2 7.6 %weights_first.1 = (bf16[2,256,256]{2,1,0:T(8,128)(2,1)}, bf16[7,2,256,256]{3,2,1,0:T(8,128)(2,1)}, bf16[512]{0:T(512)(128)(2,1)}) custom-call(s32[7]{0:T(128)} %refs_0_.3, bf16[256,512]{1,0:T(8,128)(2,1)} %refs_1_.1, bf16[768,512]{1,0:T(8,128)(2,1)} %feature_rows.1.refs_2_, bf16[512,512]{1,0:T(8,128)(2,1)} %copy-done.14, ...), custom_call_target="tpu_custom_call" | custom-call | flops 2147483648 | bytes 17564672 | tf_op jit(solution)/shard_map/weights_first/pallas_call | solution.py:312
  175.8 4.6 %output_and_grad_features.1 = (bf16[256,512]{1,0:T(8,128)(2,1)}, bf16[256,512]{1,0:T(8,128)(2,1)}) custom-call(s32[7]{0:T(128)} %refs_0_.3, bf16[512,512]{1,0:T(8,128)(2,1)} %get-tuple-element.109.hidden.refs_4_.refs_1_, bf16[512,512]{1,0:T(8,128)(2,1)} %collective-permute-done.16.refs_0_.refs_6_, bf16[512,512]{1,0:T(8,128)(2,1)} %collective-permute-done.14.refs_1_.refs_7_, ...), custom_call_target="tpu_custom_call" | custom-call | flops 536870912 | bytes 6815744 | tf_op jit(solution)/shard_map/output_and_grad_features/pallas_call | solution.py:312
  181.9 7.6 %weights_second.1 = (bf16[2,256,256]{2,1,0:T(8,128)(2,1)}, bf16[7,2,256,256]{3,2,1,0:T(8,128)(2,1)}, bf16[512]{0:T(512)(128)(2,1)}) custom-call(s32[7]{0:T(128)} %refs_0_.3, bf16[512,512]{1,0:T(8,128)(2,1)} %get-tuple-element.109.hidden.refs_4_.refs_1_, bf16[768,512]{1,0:T(8,128)(2,1)} %get-tuple-element.135.refs_2_, ...), custom_call_target="tpu_custom_call" | custom-call | flops 2147483648 | bytes 17302528 | tf_op jit(solution)/shard_map/weights_second/pallas_call | solution.py:312
  (87 shorter events, 15.1 us)
Async XLA Ops:
  7.2 119.3 %all-gather.2.cloned.1.call-start = ((), (), s32[]{:S(2)}) async-start(), calls=%async_computation | async-start | bytes 4718592 | tf_op jit(solution)/shard_map/all_gather | solution.py:411
  7.2 11.8 %collective-permute-start.1 = (bf16[256,512]{1,0:T(8,128)(2,1)}, bf16[256,512]{1,0:T(8,128)(2,1)S(1)}, u32[]{:S(2)}, u32[]{:S(2)}) collective-permute-start(bf16[256,512]{1,0:T(8,128)(2,1)} %refs_1_.1), channel_id=1, source_target_pairs={{0,200},{1,201},{2,202},{3,203},{4,204},{5,205},{6,206},{7,207},{8... | collective-permute-start | bytes 786440 | tf_op jit(solution)/shard_map/ppermute | solution.py:58
  13.7 8.3 %collective-permute-start = (bf16[256,512]{1,0:T(8,128)(2,1)}, bf16[256,512]{1,0:T(8,128)(2,1)S(1)}, u32[]{:S(2)}, u32[]{:S(2)}) collective-permute-start(bf16[256,512]{1,0:T(8,128)(2,1)} %refs_1_.1), channel_id=1, source_target_pairs={{0,64},{1,65},{2,66},{3,67},{4,68},{5,69},{6,70},{7,71},{8,72},{9,... | collective-permute-start | bytes 786440 | tf_op jit(solution)/shard_map/ppermute | solution.py:58
  22.0 8.3 %collective-permute-start.2 = (bf16[512,512]{1,0:T(8,128)(2,1)}, bf16[512,512]{1,0:T(8,128)(2,1)S(1)}, u32[]{:S(2)}, u32[]{:S(2)}) collective-permute-start(bf16[512,512]{1,0:T(8,128)(2,1)} %get-tuple-element.93), channel_id=1, source_target_pairs={{0,1},{1,0},{2,3},{3,2},{4,5},{5,4},{6,7},{7,6},{8,9},{9,8},{10,11... | collective-permute-start | bytes 1572872 | tf_op jit(solution)/shard_map/ppermute | solution.py:33
  23.9 13.8 %collective-permute-start.3 = (bf16[512,512]{1,0:T(8,128)(2,1)}, bf16[512,512]{1,0:T(8,128)(2,1)S(1)}, u32[]{:S(2)}, u32[]{:S(2)}) collective-permute-start(bf16[512,512]{1,0:T(8,128)(2,1)} %get-tuple-element.94), channel_id=1, source_target_pairs={{0,2},{1,3},{2,0},{3,1},{4,6},{5,7},{6,4},{7,5},{8,10},{9,11},{10,... | collective-permute-start | bytes 1572872 | tf_op jit(solution)/shard_map/ppermute | solution.py:33
  25.1 26.0 %collective-permute-start.4 = (bf16[512,512]{1,0:T(8,128)(2,1)}, bf16[512,512]{1,0:T(8,128)(2,1)S(1)}, u32[]{:S(2)}, u32[]{:S(2)}) collective-permute-start(bf16[512,512]{1,0:T(8,128)(2,1)} %get-tuple-element.95), channel_id=1, source_target_pairs={{0,4},{1,5},{2,6},{3,7},{4,0},{5,1},{6,2},{7,3},{8,12},{9,13},{10,... | collective-permute-start | bytes 1572872 | tf_op jit(solution)/shard_map/ppermute | solution.py:33
  27.5 28.7 %collective-permute-start.5 = (bf16[512,512]{1,0:T(8,128)(2,1)}, bf16[512,512]{1,0:T(8,128)(2,1)S(1)}, u32[]{:S(2)}, u32[]{:S(2)}) collective-permute-start(bf16[512,512]{1,0:T(8,128)(2,1)} %get-tuple-element.96), channel_id=1, source_target_pairs={{0,8},{1,9},{2,10},{3,11},{4,12},{5,13},{6,14},{7,15},{8,0},{9,1},... | collective-permute-start | bytes 1572872 | tf_op jit(solution)/shard_map/ppermute | solution.py:33
  28.9 27.3 %collective-permute-start.6 = (bf16[512,512]{1,0:T(8,128)(2,1)}, bf16[512,512]{1,0:T(8,128)(2,1)S(1)}, u32[]{:S(2)}, u32[]{:S(2)}) collective-permute-start(bf16[512,512]{1,0:T(8,128)(2,1)} %get-tuple-element.97), channel_id=1, source_target_pairs={{0,16},{1,17},{2,18},{3,19},{4,20},{5,21},{6,22},{7,23},{8,24},{9,... | collective-permute-start | bytes 1572872 | tf_op jit(solution)/shard_map/ppermute | solution.py:33
  30.2 26.0 %collective-permute-start.7 = (bf16[512,512]{1,0:T(8,128)(2,1)}, bf16[512,512]{1,0:T(8,128)(2,1)S(1)}, u32[]{:S(2)}, u32[]{:S(2)}) collective-permute-start(bf16[512,512]{1,0:T(8,128)(2,1)} %get-tuple-element.98), channel_id=1, source_target_pairs={{0,32},{1,33},{2,34},{3,35},{4,36},{5,37},{6,38},{7,39},{8,40},{9,... | collective-permute-start | bytes 1572872 | tf_op jit(solution)/shard_map/ppermute | solution.py:33
  57.5 12.9 %collective-permute-start.9 = (bf16[512,512]{1,0:T(8,128)(2,1)}, bf16[512,512]{1,0:T(8,128)(2,1)S(1)}, u32[]{:S(2)}, u32[]{:S(2)}) collective-permute-start(bf16[512,512]{1,0:T(8,128)(2,1)} %get-tuple-element.161), channel_id=1, source_target_pairs={{0,200},{1,201},{2,202},{3,203},{4,204},{5,205},{6,206},{7,207},{8... | collective-permute-start | bytes 1572872 | tf_op jit(solution)/shard_map/ppermute | solution.py:58
  57.5 13.8 %collective-permute-start.8 = (bf16[512,512]{1,0:T(8,128)(2,1)}, bf16[512,512]{1,0:T(8,128)(2,1)S(1)}, u32[]{:S(2)}, u32[]{:S(2)}) collective-permute-start(bf16[512,512]{1,0:T(8,128)(2,1)} %get-tuple-element.162), channel_id=1, source_target_pairs={{0,64},{1,65},{2,66},{3,67},{4,68},{5,69},{6,70},{7,71},{8,72},{9,... | collective-permute-start | bytes 1572872 | tf_op jit(solution)/shard_map/ppermute | solution.py:58
  71.4 14.5 %collective-permute-start.10 = (bf16[512,512]{1,0:T(8,128)(2,1)S(1)}, bf16[512,512]{1,0:T(8,128)(2,1)S(1)}, u32[]{:S(2)}, u32[]{:S(2)}) collective-permute-start(bf16[512,512]{1,0:T(8,128)(2,1)S(1)} %collective-permute-done.8.refs_1_.refs_17_.refs_16_), channel_id=1, source_target_pairs={{0,64},{1,65},{2,66},{3,67},{4,68},{5,69},{6,70},{7,71},{8,72},{9,... | collective-permute-start | bytes 1572872 | tf_op jit(solution)/shard_map/ppermute | solution.py:58
  71.7 16.0 %collective-permute-start.11 = (bf16[512,512]{1,0:T(8,128)(2,1)S(1)}, bf16[512,512]{1,0:T(8,128)(2,1)S(1)}, u32[]{:S(2)}, u32[]{:S(2)}) collective-permute-start(bf16[512,512]{1,0:T(8,128)(2,1)S(1)} %collective-permute-done.9.refs_4_.refs_20_.refs_19_), channel_id=1, source_target_pairs={{0,200},{1,201},{2,202},{3,203},{4,204},{5,205},{6,206},{7,207},{8... | collective-permute-start | bytes 1572872 | tf_op jit(solution)/shard_map/ppermute | solution.py:58
  74.1 27.3 %collective-permute-start.12 = (bf16[512,512]{1,0:T(8,128)(2,1)}, bf16[512,512]{1,0:T(8,128)(2,1)S(1)}, u32[]{:S(2)}, u32[]{:S(2)}) collective-permute-start(bf16[512,512]{1,0:T(8,128)(2,1)} %get-tuple-element.116), channel_id=1, source_target_pairs={{0,4},{1,5},{2,6},{3,7},{4,0},{5,1},{6,2},{7,3},{8,12},{9,13},{10,... | collective-permute-start | bytes 1572872 | tf_op jit(solution)/shard_map/ppermute | solution.py:33
  74.6 26.8 %collective-permute-start.13 = (bf16[512,512]{1,0:T(8,128)(2,1)}, bf16[512,512]{1,0:T(8,128)(2,1)S(1)}, u32[]{:S(2)}, u32[]{:S(2)}) collective-permute-start(bf16[512,512]{1,0:T(8,128)(2,1)} %get-tuple-element.117), channel_id=1, source_target_pairs={{0,32},{1,33},{2,34},{3,35},{4,36},{5,37},{6,38},{7,39},{8,40},{9,... | collective-permute-start | bytes 1572872 | tf_op jit(solution)/shard_map/ppermute | solution.py:33
  78.2 26.2 %collective-permute-start.14 = (bf16[512,512]{1,0:T(8,128)(2,1)}, bf16[512,512]{1,0:T(8,128)(2,1)}, u32[]{:S(2)}, u32[]{:S(2)}) collective-permute-start(bf16[512,512]{1,0:T(8,128)(2,1)} %get-tuple-element.120), channel_id=1, source_target_pairs={{0,2},{1,3},{2,0},{3,1},{4,6},{5,7},{6,4},{7,5},{8,10},{9,11},{10,... | collective-permute-start | bytes 1572872 | tf_op jit(solution)/shard_map/ppermute | solution.py:33
  87.7 16.7 %collective-permute-start.15 = (bf16[512,512]{1,0:T(8,128)(2,1)}, bf16[512,512]{1,0:T(8,128)(2,1)}, u32[]{:S(2)}, u32[]{:S(2)}) collective-permute-start(bf16[512,512]{1,0:T(8,128)(2,1)} %get-tuple-element.121), channel_id=1, source_target_pairs={{0,16},{1,17},{2,18},{3,19},{4,20},{5,21},{6,22},{7,23},{8,24},{9,... | collective-permute-start | bytes 1572872 | tf_op jit(solution)/shard_map/ppermute | solution.py:33
  91.6 12.8 %collective-permute-start.16 = (bf16[512,512]{1,0:T(8,128)(2,1)}, bf16[512,512]{1,0:T(8,128)(2,1)}, u32[]{:S(2)}, u32[]{:S(2)}) collective-permute-start(bf16[512,512]{1,0:T(8,128)(2,1)} %get-tuple-element.122), channel_id=1, source_target_pairs={{0,1},{1,0},{2,3},{3,2},{4,5},{5,4},{6,7},{7,6},{8,9},{9,8},{10,11... | collective-permute-start | bytes 1572872 | tf_op jit(solution)/shard_map/ppermute | solution.py:33
  101.4 63.3 %copy-start.3 = (bf16[512,512]{1,0:T(8,128)(2,1)S(1)}, bf16[512,512]{1,0:T(8,128)(2,1)}, u32[]{:S(2)}) copy-start(bf16[512,512]{1,0:T(8,128)(2,1)} %copy-done.2) | copy-start | bytes 1572868
  101.5 21.5 %collective-permute-start.18 = (bf16[768,512]{1,0:T(8,128)(2,1)}, bf16[768,512]{1,0:T(8,128)(2,1)S(1)}, u32[]{:S(2)}, u32[]{:S(2)}) collective-permute-start(bf16[768,512]{1,0:T(8,128)(2,1)} %feature_rows.1.refs_2_), channel_id=1, source_target_pairs={{0,32},{1,33},{2,34},{3,35},{4,36},{5,37},{6,38},{7,39},{8,40},{9,... | collective-permute-start | bytes 2359304 | tf_op jit(solution)/shard_map/ppermute | solution.py:33
  104.4 20.7 %collective-permute-start.17 = (bf16[768,512]{1,0:T(8,128)(2,1)}, bf16[768,512]{1,0:T(8,128)(2,1)}, u32[]{:S(2)}, u32[]{:S(2)}) collective-permute-start(bf16[768,512]{1,0:T(8,128)(2,1)} %feature_rows.1.refs_2_), channel_id=1, source_target_pairs={{0,4},{1,5},{2,6},{3,7},{4,0},{5,1},{6,2},{7,3},{8,12},{9,13},{10,... | collective-permute-start | bytes 2359304 | tf_op jit(solution)/shard_map/ppermute | solution.py:33
  104.4 25.0 %collective-permute-start.21 = (bf16[768,512]{1,0:T(8,128)(2,1)}, bf16[768,512]{1,0:T(8,128)(2,1)}, u32[]{:S(2)}, u32[]{:S(2)}) collective-permute-start(bf16[768,512]{1,0:T(8,128)(2,1)} %feature_rows.1.refs_2_), channel_id=1, source_target_pairs={{0,1},{1,0},{2,3},{3,2},{4,5},{5,4},{6,7},{7,6},{8,9},{9,8},{10,11... | collective-permute-start | bytes 2359304 | tf_op jit(solution)/shard_map/ppermute | solution.py:33
  106.2 32.8 %collective-permute-start.20 = (bf16[768,512]{1,0:T(8,128)(2,1)}, bf16[768,512]{1,0:T(8,128)(2,1)}, u32[]{:S(2)}, u32[]{:S(2)}) collective-permute-start(bf16[768,512]{1,0:T(8,128)(2,1)} %feature_rows.1.refs_2_), channel_id=1, source_target_pairs={{0,16},{1,17},{2,18},{3,19},{4,20},{5,21},{6,22},{7,23},{8,24},{9,... | collective-permute-start | bytes 2359304 | tf_op jit(solution)/shard_map/ppermute | solution.py:33
  107.9 31.1 %collective-permute-start.19 = (bf16[768,512]{1,0:T(8,128)(2,1)}, bf16[768,512]{1,0:T(8,128)(2,1)}, u32[]{:S(2)}, u32[]{:S(2)}) collective-permute-start(bf16[768,512]{1,0:T(8,128)(2,1)} %feature_rows.1.refs_2_), channel_id=1, source_target_pairs={{0,2},{1,3},{2,0},{3,1},{4,6},{5,7},{6,4},{7,5},{8,10},{9,11},{10,... | collective-permute-start | bytes 2359304 | tf_op jit(solution)/shard_map/ppermute | solution.py:33
  139.0 5.0 %collective-permute-start.22 = (bf16[768,512]{1,0:T(8,128)(2,1)}, bf16[768,512]{1,0:T(8,128)(2,1)S(1)}, u32[]{:S(2)}, u32[]{:S(2)}) collective-permute-start(bf16[768,512]{1,0:T(8,128)(2,1)} %get-tuple-element.135.refs_2_), channel_id=1, source_target_pairs={{0,1},{1,0},{2,3},{3,2},{4,5},{5,4},{6,7},{7,6},{8,9},{9,8},{10,11... | collective-permute-start | bytes 2359304 | tf_op jit(solution)/shard_map/ppermute | solution.py:33
  139.9 21.6 %collective-permute-start.26 = (bf16[768,512]{1,0:T(8,128)(2,1)}, bf16[768,512]{1,0:T(8,128)(2,1)S(1)}, u32[]{:S(2)}, u32[]{:S(2)}) collective-permute-start(bf16[768,512]{1,0:T(8,128)(2,1)} %get-tuple-element.135.refs_2_), channel_id=1, source_target_pairs={{0,32},{1,33},{2,34},{3,35},{4,36},{5,37},{6,38},{7,39},{8,40},{9,... | collective-permute-start | bytes 2359304 | tf_op jit(solution)/shard_map/ppermute | solution.py:33
  143.3 20.6 %collective-permute-start.25 = (bf16[768,512]{1,0:T(8,128)(2,1)}, bf16[768,512]{1,0:T(8,128)(2,1)S(1)}, u32[]{:S(2)}, u32[]{:S(2)}) collective-permute-start(bf16[768,512]{1,0:T(8,128)(2,1)} %get-tuple-element.135.refs_2_), channel_id=1, source_target_pairs={{0,4},{1,5},{2,6},{3,7},{4,0},{5,1},{6,2},{7,3},{8,12},{9,13},{10,... | collective-permute-start | bytes 2359304 | tf_op jit(solution)/shard_map/ppermute | solution.py:33
  143.3 37.1 %collective-permute-start.27 = (bf16[768,512]{1,0:T(8,128)(2,1)}, bf16[768,512]{1,0:T(8,128)(2,1)}, u32[]{:S(2)}, u32[]{:S(2)}) collective-permute-start(bf16[768,512]{1,0:T(8,128)(2,1)} %get-tuple-element.135.refs_2_), channel_id=1, source_target_pairs={{0,16},{1,17},{2,18},{3,19},{4,20},{5,21},{6,22},{7,23},{8,24},{9,... | collective-permute-start | bytes 2359304 | tf_op jit(solution)/shard_map/ppermute | solution.py:33
  143.9 36.6 %collective-permute-start.24 = (bf16[768,512]{1,0:T(8,128)(2,1)}, bf16[768,512]{1,0:T(8,128)(2,1)}, u32[]{:S(2)}, u32[]{:S(2)}) collective-permute-start(bf16[768,512]{1,0:T(8,128)(2,1)} %get-tuple-element.135.refs_2_), channel_id=1, source_target_pairs={{0,2},{1,3},{2,0},{3,1},{4,6},{5,7},{6,4},{7,5},{8,10},{9,11},{10,... | collective-permute-start | bytes 2359304 | tf_op jit(solution)/shard_map/ppermute | solution.py:33
  144.0 31.8 %collective-permute-start.23 = (bf16[256,512]{1,0:T(8,128)(2,1)}, bf16[256,512]{1,0:T(8,128)(2,1)}, u32[]{:S(2)}, u32[]{:S(2)}) collective-permute-start(bf16[256,512]{1,0:T(8,128)(2,1)} %get-tuple-element.136), channel_id=1, source_target_pairs={{0,8},{1,9},{2,10},{3,11},{4,12},{5,13},{6,14},{7,15},{8,0},{9,1},... | collective-permute-start | bytes 786440 | tf_op jit(solution)/shard_map/ppermute | solution.py:33
  164.7 15.7 %collective-permute-start.29 = (bf16[256,512]{1,0:T(8,128)(2,1)S(1)}, bf16[256,512]{1,0:T(8,128)(2,1)S(1)}, u32[]{:S(2)}, u32[]{:S(2)}) collective-permute-start(bf16[256,512]{1,0:T(8,128)(2,1)S(1)} %slice.7), channel_id=1, source_target_pairs={{0,200},{1,201},{2,202},{3,203},{4,204},{5,205},{6,206},{7,207},{8... | collective-permute-start | bytes 786440 | tf_op jit(solution)/shard_map/ppermute | solution.py:58
  168.2 12.3 %collective-permute-start.28 = (bf16[256,512]{1,0:T(8,128)(2,1)}, bf16[256,512]{1,0:T(8,128)(2,1)S(1)}, u32[]{:S(2)}, u32[]{:S(2)}) collective-permute-start(bf16[256,512]{1,0:T(8,128)(2,1)} %slice.6), channel_id=1, source_target_pairs={{0,64},{1,65},{2,66},{3,67},{4,68},{5,69},{6,70},{7,71},{8,72},{9,... | collective-permute-start | bytes 786440 | tf_op jit(solution)/shard_map/ppermute | solution.py:58
  (22 other events, 465.9 us)
Sparse Core Ops, SparseCore 0:
  71.5 54.9 all-gather.1

commit v2 on v1

--- a/solution.py
+++ b/solution.py
@@ -16,7 +16,7 @@
 DEVICE_BITS = 6
 FEAT = ("y", "z_hi", "x_core")
 NEAR = (CORE, X1, X2, Y1, Y2)
-START_ORDER = (ZHI, X2, Y2, CORE, X1, Y1)
+START_ORDER = (X2, Y2, X1, Y1, ZHI, CORE)
 SQRT_2_OVER_PI = 0.7978845608028654
 CUBIC = 0.044715
 VMEM_LIMIT = 60 * 1024 * 1024
@@ -436,10 +436,6 @@
     hidden_near.update(send({X1: hidden_rows, Y1: hidden_rows, CORE: hidden_rows}))
     far_product, hidden_near[CORE] = after(sent[ZHI], hidden_near[CORE])
     got_late[ZHI] = from_partner(far_product, ZHI)
-    up, down, hidden_near[X2], hidden_near[Y2] = after(
-        *features_z[2], hidden_near[X2], hidden_near[Y2]
-    )
-    grad_z = [*features_z[1:], both_ways(up[ROWS:], down[ROWS:])]
     diag_first_grad, part_first_grad, bias_grad = weight_sums(
         "weights_first",
         section_bit,
@@ -455,6 +451,8 @@
             *chunks_of(features_z),
         ),
     )
+    up, down, bias_grad = after(*[value[ROWS:] for value in features_z[2]], bias_grad)
+    grad_z = [*features_z[1:], both_ways(up, down)]
     output, grad_in = call(
         last_kernel,
         "output_and_grad_features",

time: 197 us -> 190 us (0.964)
  waiting for transfers between devices: 90.7 us -> 80.1 us
  starting transfers between devices: 51.9 us -> 56.4 us
    ppermute x22, waiting for transfers between devices: 69.9 us -> 59.4 us  [from_partner(): return lax.ppermute(value, FEAT, pairs)]
    ppermute x8, waiting for transfers between devices: 19.3 us -> 13.7 us  [along_z(): return lax.ppermute(value, ('dp', *FEAT), pairs)]
    all_gather x1, waiting for transfers between devices: 1.43 us -> 7.01 us  [on_device(): gathered = lax.all_gather(late, ('z_hi', 'dp'), axis=0, tiled=True)]
    ppermute x22, starting transfers between devices: 37.6 us -> 41.7 us  [from_partner(): return lax.ppermute(value, FEAT, pairs)]
  transfers between devices with their start and end apart: 31 -> 31, of which waited for: 15 -> 16; matrix products, arithmetic and copies ran while one was open for 0% -> 0% of each run, Pallas kernels for 14% -> 15%
where the time goes in v2:
time: 190 us
  waiting for transfers between devices  80.1 us (42%)
  starting transfers between devices  56.4 us (30%)
  Pallas kernels  35.9 us (19%)
  between operations  14.3 us (8%)
  local copies, waits for them, and re-layouts  2.26 us (1%)
    ppermute x22, waiting for transfers between devices, from_partner(): return lax.ppermute(value, FEAT, pairs)  59.4 us
    ppermute x22, starting transfers between devices, from_partner(): return lax.ppermute(value, FEAT, pairs)  41.7 us
    pallas_call x7, Pallas kernels, call(): pl.pallas_call(kernel, grid=(1,), out_shape=out_shape, in_specs=[SCALARS]...  35.9 us
    ppermute x8, starting transfers between devices, along_z(): return lax.ppermute(value, ('dp', *FEAT), pairs)  14.6 us
    ppermute x8, waiting for transfers between devices, along_z(): return lax.ppermute(value, ('dp', *FEAT), pairs)  13.7 us
    all_gather x1, waiting for transfers between devices, on_device(): gathered = lax.all_gather(late, ('z_hi', 'dp'), axis=0, tiled=True)  7.01 us
  transfers between devices with their start and end apart: 31, of which 16 were waited for; matrix products, arithmetic and copies ran while one was open for 0% of the time, Pallas kernels for 15%

profile of v2, /device:TPU:1, one launch (start us, length us, event | category | flops | bytes accessed | tf_op | source)
XLA Modules:
  0.0 190.1 jit_solution(6242439675948394394)
XLA Ops:
  7.2 2.5 %collective-permute-start = (bf16[256,512]{1,0:T(8,128)(2,1)}, bf16[256,512]{1,0:T(8,128)(2,1)S(1)}, u32[]{:S(2)}, u32[]{:S(2)}) collective-permute-start(bf16[256,512]{1,0:T(8,128)(2,1)} %refs_1_.1), channel_id=1, source_target_pairs={{0,64},{1,65},{2,66},{3,67},{4,68},{5,69},{6,70},{7,71},{8,72},{9,... | collective-permute-start | bytes 786440 | tf_op jit(solution)/shard_map/ppermute | solution.py:58
  9.8 4.0 %collective-permute-start.1 = (bf16[256,512]{1,0:T(8,128)(2,1)}, bf16[256,512]{1,0:T(8,128)(2,1)S(1)}, u32[]{:S(2)}, u32[]{:S(2)}) collective-permute-start(bf16[256,512]{1,0:T(8,128)(2,1)} %refs_1_.1), channel_id=1, source_target_pairs={{0,200},{1,201},{2,202},{3,203},{4,204},{5,205},{6,206},{7,207},{8... | collective-permute-start | bytes 786440 | tf_op jit(solution)/shard_map/ppermute | solution.py:58
  13.8 4.2 %products_second.1 = (f32[256,512]{1,0:T(8,128)}, bf16[512,512]{1,0:T(8,128)(2,1)}, bf16[512,512]{1,0:T(8,128)(2,1)}, bf16[512,512]{1,0:T(8,128)(2,1)}, bf16[512...) custom-call(s32[7]{0:T(128)} %refs_0_.3, bf16[256,512]{1,0:T(8,128)(2,1)} %refs_1_.1, ...), custom_call_target="tpu_custom_call" | custom-call | flops 536870912 | bytes 6291456 | tf_op jit(solution)/shard_map/products_second/pallas_call | solution.py:312
  22.5 2.5 %collective-permute-start.4 = (bf16[512,512]{1,0:T(8,128)(2,1)}, bf16[512,512]{1,0:T(8,128)(2,1)S(1)}, u32[]{:S(2)}, u32[]{:S(2)}) collective-permute-start(bf16[512,512]{1,0:T(8,128)(2,1)} %get-tuple-element.94), channel_id=1, source_target_pairs={{0,4},{1,5},{2,6},{3,7},{4,0},{5,1},{6,2},{7,3},{8,12},{9,13},{10,... | collective-permute-start | bytes 1572872 | tf_op jit(solution)/shard_map/ppermute | solution.py:33
  24.9 4.0 %collective-permute-start.5 = (bf16[512,512]{1,0:T(8,128)(2,1)}, bf16[512,512]{1,0:T(8,128)(2,1)S(1)}, u32[]{:S(2)}, u32[]{:S(2)}) collective-permute-start(bf16[512,512]{1,0:T(8,128)(2,1)} %get-tuple-element.95), channel_id=1, source_target_pairs={{0,8},{1,9},{2,10},{3,11},{4,12},{5,13},{6,14},{7,15},{8,0},{9,1},... | collective-permute-start | bytes 1572872 | tf_op jit(solution)/shard_map/ppermute | solution.py:33
  30.3 2.6 %collective-permute-start.7 = (bf16[512,512]{1,0:T(8,128)(2,1)}, bf16[512,512]{1,0:T(8,128)(2,1)S(1)}, u32[]{:S(2)}, u32[]{:S(2)}) collective-permute-start(bf16[512,512]{1,0:T(8,128)(2,1)} %get-tuple-element.97), channel_id=1, source_target_pairs={{0,32},{1,33},{2,34},{3,35},{4,36},{5,37},{6,38},{7,39},{8,40},{9,... | collective-permute-start | bytes 1572872 | tf_op jit(solution)/shard_map/ppermute | solution.py:33
  32.9 2.1 %collective-permute-done.3.refs_1_.refs_7_ = bf16[512,512]{1,0:T(8,128)(2,1)S(1)} collective-permute-done((bf16[512,512]{1,0:T(8,128)(2,1)}, bf16[512,512]{1,0:T(8,128)(2,1)S(1)}, u32[]{:S(2)}, u32[]{:S(2)}) %collective-permute-start.3) | collective-permute-done | bytes 524320 | tf_op jit(solution)/shard_map/ppermute | solution.py:33
  35.0 13.4 %collective-permute-done.4.refs_2_.refs_8_ = bf16[512,512]{1,0:T(8,128)(2,1)S(1)} collective-permute-done((bf16[512,512]{1,0:T(8,128)(2,1)}, bf16[512,512]{1,0:T(8,128)(2,1)S(1)}, u32[]{:S(2)}, u32[]{:S(2)}) %collective-permute-start.4) | collective-permute-done | bytes 524320 | tf_op jit(solution)/shard_map/ppermute | solution.py:33
  48.4 6.9 %collective-permute-done.7.refs_5_.refs_10_ = bf16[512,512]{1,0:T(8,128)(2,1)S(1)} collective-permute-done((bf16[512,512]{1,0:T(8,128)(2,1)}, bf16[512,512]{1,0:T(8,128)(2,1)S(1)}, u32[]{:S(2)}, u32[]{:S(2)}) %collective-permute-start.7) | collective-permute-done | bytes 524320 | tf_op jit(solution)/shard_map/ppermute | solution.py:33
  56.8 2.5 %collective-permute-start.9 = (bf16[512,512]{1,0:T(8,128)(2,1)}, bf16[512,512]{1,0:T(8,128)(2,1)S(1)}, u32[]{:S(2)}, u32[]{:S(2)}) collective-permute-start(bf16[512,512]{1,0:T(8,128)(2,1)} %get-tuple-element.159), channel_id=1, source_target_pairs={{0,200},{1,201},{2,202},{3,203},{4,204},{5,205},{6,206},{7,207},{8... | collective-permute-start | bytes 1572872 | tf_op jit(solution)/shard_map/ppermute | solution.py:58
  59.3 6.3 %hidden_and_grad_pre.1 = (bf16[512,512]{1,0:T(8,128)(2,1)}, f32[256,512]{1,0:T(8,128)}, bf16[512,512]{1,0:T(8,128)(2,1)}, bf16[512,512]{1,0:T(8,128)(2,1)}, bf16...) custom-call(s32[7]{0:T(128)} %refs_0_.3, ...), custom_call_target="tpu_custom_call" | custom-call | flops 1073741824 | bytes 9962496 | tf_op jit(solution)/shard_map/hidden_and_grad_pre/pallas_call | solution.py:312
  65.6 3.9 %collective-permute-done.8.refs_1_.refs_17_.refs_16_ = bf16[512,512]{1,0:T(8,128)(2,1)S(1)} collective-permute-done((bf16[512,512]{1,0:T(8,128)(2,1)}, bf16[512,512]{1,0:T(8,128)(2,1)S(1)}, u32[]{:S(2)}, u32[]{:S(2)}) %collective-permute-start.8) | collective-permute-done | bytes 524320 | tf_op jit(solution)/shard_map/ppermute | solution.py:58
  72.8 2.4 %collective-permute-start.13 = (bf16[512,512]{1,0:T(8,128)(2,1)}, bf16[512,512]{1,0:T(8,128)(2,1)S(1)}, u32[]{:S(2)}, u32[]{:S(2)}) collective-permute-start(bf16[512,512]{1,0:T(8,128)(2,1)} %get-tuple-element.116), channel_id=1, source_target_pairs={{0,32},{1,33},{2,34},{3,35},{4,36},{5,37},{6,38},{7,39},{8,40},{9,... | collective-permute-start | bytes 1572872 | tf_op jit(solution)/shard_map/ppermute | solution.py:33
  75.5 6.0 %collective-permute-done.10.refs_2_.refs_18_.refs_17_ = bf16[512,512]{1,0:T(8,128)(2,1)S(1)} collective-permute-done((bf16[512,512]{1,0:T(8,128)(2,1)S(1)}, bf16[512,512]{1,0:T(8,128)(2,1)S(1)}, u32[]{:S(2)}, u32[]{:S(2)}) %collective-permute-start.10) | collective-permute-done | bytes 524320 | tf_op jit(solution)/shard_map/ppermute | solution.py:58
  83.3 3.4 %collective-permute-start.15 = (bf16[512,512]{1,0:T(8,128)(2,1)}, bf16[512,512]{1,0:T(8,128)(2,1)}, u32[]{:S(2)}, u32[]{:S(2)}) collective-permute-start(bf16[512,512]{1,0:T(8,128)(2,1)} %get-tuple-element.120), channel_id=1, source_target_pairs={{0,16},{1,17},{2,18},{3,19},{4,20},{5,21},{6,22},{7,23},{8,24},{9,... | collective-permute-start | bytes 1572872 | tf_op jit(solution)/shard_map/ppermute | solution.py:33
  86.7 7.0 %collective-permute-start.16 = (bf16[512,512]{1,0:T(8,128)(2,1)}, bf16[512,512]{1,0:T(8,128)(2,1)}, u32[]{:S(2)}, u32[]{:S(2)}) collective-permute-start(bf16[512,512]{1,0:T(8,128)(2,1)} %get-tuple-element.121), channel_id=1, source_target_pairs={{0,1},{1,0},{2,3},{3,2},{4,5},{5,4},{6,7},{7,6},{8,9},{9,8},{10,11... | collective-permute-start | bytes 1572872 | tf_op jit(solution)/shard_map/ppermute | solution.py:33
  93.7 2.7 %feature_rows.1.refs_2_ = bf16[768,512]{1,0:T(8,128)(2,1)} custom-call(s32[7]{0:T(128)} %refs_0_.3, bf16[256,512]{1,0:T(8,128)(2,1)} %copy-done.6, bf16[512,512]{1,0:T(8,128)(2,1)} %copy-done.4, bf16[512,512]{1,0:T(8,128)(2,1)} %copy-done, bf16[256,512]{1,0:T(8,128)(2,1)} %copy-done.7, bf16[512,512]{1,0:T(8,128)(2,1)} %copy-done.5, bf16[512,512]{1,0:T(8,128)(2,1)} %copy-done.2), custom_call_target="tpu_custom_call" | custom-call | bytes 3407872 | tf_op jit(solution)/shard_map/feature_rows/pallas_call | solution.py:312
  96.6 2.9 %collective-permute-start.18 = (bf16[768,512]{1,0:T(8,128)(2,1)}, bf16[768,512]{1,0:T(8,128)(2,1)}, u32[]{:S(2)}, u32[]{:S(2)}) collective-permute-start(bf16[768,512]{1,0:T(8,128)(2,1)} %feature_rows.1.refs_2_), channel_id=1, source_target_pairs={{0,32},{1,33},{2,34},{3,35},{4,36},{5,37},{6,38},{7,39},{8,40},{9,... | collective-permute-start | bytes 2359304 | tf_op jit(solution)/shard_map/ppermute | solution.py:33
  99.7 3.5 %collective-permute-start.21 = (bf16[768,512]{1,0:T(8,128)(2,1)}, bf16[768,512]{1,0:T(8,128)(2,1)}, u32[]{:S(2)}, u32[]{:S(2)}) collective-permute-start(bf16[768,512]{1,0:T(8,128)(2,1)} %feature_rows.1.refs_2_), channel_id=1, source_target_pairs={{0,1},{1,0},{2,3},{3,2},{4,5},{5,4},{6,7},{7,6},{8,9},{9,8},{10,11... | collective-permute-start | bytes 2359304 | tf_op jit(solution)/shard_map/ppermute | solution.py:33
  103.2 14.3 %collective-permute-done.17.refs_13_ = bf16[768,512]{1,0:T(8,128)(2,1)S(1)} collective-permute-done((bf16[768,512]{1,0:T(8,128)(2,1)}, bf16[768,512]{1,0:T(8,128)(2,1)S(1)}, u32[]{:S(2)}, u32[]{:S(2)}) %collective-permute-start.17) | collective-permute-done | bytes 786464 | tf_op jit(solution)/shard_map/ppermute | solution.py:33
  118.1 7.0 %all-gather.2.cloned.1.call-done.gathered.refs_5_ = bf16[4096,512]{1,0:T(8,128)(2,1)} async-done(((bf16[512,512]{1,0:T(8,128)(2,1)}), bf16[4096,512]{1,0:T(8,128)(2,1)}) %all-gather.2.cloned.1.call-update) | async-done | bytes 4194320 | tf_op jit(solution)/shard_map/all_gather | solution.py:411
  125.1 2.9 %hidden_rows.1 = (bf16[768,512]{1,0:T(8,128)(2,1)}, bf16[256,512]{1,0:T(8,128)(2,1)}) custom-call(s32[7]{0:T(128)} %refs_0_.3, bf16[4096,512]{1,0:T(8,128)(2,1)} %all-gather.2.cloned.1.call-done.gathered.refs_5_), custom_call_target="tpu_custom_call" | custom-call | bytes 5242880 | tf_op jit(solution)/shard_map/hidden_rows/pallas_call | solution.py:312
  128.0 2.8 %collective-permute-done.19.refs_12_ = bf16[768,512]{1,0:T(8,128)(2,1)} collective-permute-done((bf16[768,512]{1,0:T(8,128)(2,1)}, bf16[768,512]{1,0:T(8,128)(2,1)}, u32[]{:S(2)}, u32[]{:S(2)}) %collective-permute-start.19) | collective-permute-done | bytes 786464 | tf_op jit(solution)/shard_map/ppermute | solution.py:33
  130.9 3.7 %collective-permute-done.20.refs_14_ = bf16[768,512]{1,0:T(8,128)(2,1)} collective-permute-done((bf16[768,512]{1,0:T(8,128)(2,1)}, bf16[768,512]{1,0:T(8,128)(2,1)}, u32[]{:S(2)}, u32[]{:S(2)}) %collective-permute-start.20) | collective-permute-done | bytes 786464 | tf_op jit(solution)/shard_map/ppermute | solution.py:33
  136.6 2.8 %collective-permute-start.25 = (bf16[768,512]{1,0:T(8,128)(2,1)}, bf16[768,512]{1,0:T(8,128)(2,1)}, u32[]{:S(2)}, u32[]{:S(2)}) collective-permute-start(bf16[768,512]{1,0:T(8,128)(2,1)} %get-tuple-element.134.refs_2_), channel_id=1, source_target_pairs={{0,4},{1,5},{2,6},{3,7},{4,0},{5,1},{6,2},{7,3},{8,12},{9,13},{10,... | collective-permute-start | bytes 2359304 | tf_op jit(solution)/shard_map/ppermute | solution.py:33
  139.9 3.3 %collective-permute-start.23 = (bf16[256,512]{1,0:T(8,128)(2,1)}, bf16[256,512]{1,0:T(8,128)(2,1)}, u32[]{:S(2)}, u32[]{:S(2)}) collective-permute-start(bf16[256,512]{1,0:T(8,128)(2,1)} %get-tuple-element.135), channel_id=1, source_target_pairs={{0,8},{1,9},{2,10},{3,11},{4,12},{5,13},{6,14},{7,15},{8,0},{9,1},... | collective-permute-start | bytes 786440 | tf_op jit(solution)/shard_map/ppermute | solution.py:33
  143.9 7.6 %weights_first.1 = (bf16[2,256,256]{2,1,0:T(8,128)(2,1)}, bf16[7,2,256,256]{3,2,1,0:T(8,128)(2,1)}, bf16[512]{0:T(512)(128)(2,1)}) custom-call(s32[7]{0:T(128)} %refs_0_.3, bf16[256,512]{1,0:T(8,128)(2,1)} %refs_1_.1, bf16[768,512]{1,0:T(8,128)(2,1)} %feature_rows.1.refs_2_, bf16[512,512]{1,0:T(8,128)(2,1)} %copy-done.14, ...), custom_call_target="tpu_custom_call" | custom-call | flops 2147483648 | bytes 17564672 | tf_op jit(solution)/shard_map/weights_first/pallas_call | solution.py:312
  151.6 3.3 %collective-permute-done.24.refs_12_ = bf16[768,512]{1,0:T(8,128)(2,1)S(1)} collective-permute-done((bf16[768,512]{1,0:T(8,128)(2,1)}, bf16[768,512]{1,0:T(8,128)(2,1)S(1)}, u32[]{:S(2)}, u32[]{:S(2)}) %collective-permute-start.24) | collective-permute-done | bytes 786464 | tf_op jit(solution)/shard_map/ppermute | solution.py:33
  155.8 2.1 %collective-permute-done.23.refs_5_ = bf16[256,512]{1,0:T(8,128)(2,1)} collective-permute-done((bf16[256,512]{1,0:T(8,128)(2,1)}, bf16[256,512]{1,0:T(8,128)(2,1)}, u32[]{:S(2)}, u32[]{:S(2)}) %collective-permute-start.23) | collective-permute-done | bytes 262176 | tf_op jit(solution)/shard_map/ppermute | solution.py:33
  159.5 4.6 %output_and_grad_features.1 = (bf16[256,512]{1,0:T(8,128)(2,1)}, bf16[256,512]{1,0:T(8,128)(2,1)}) custom-call(s32[7]{0:T(128)} %refs_0_.3, bf16[512,512]{1,0:T(8,128)(2,1)} %get-tuple-element.108.hidden.refs_4_.refs_1_, bf16[512,512]{1,0:T(8,128)(2,1)} %collective-permute-done.16.refs_0_.refs_6_, bf16[512,512]{1,0:T(8,128)(2,1)} %collective-permute-done.14.refs_1_.refs_7_, ...), custom_call_target="tpu_custom_call" | custom-call | flops 536870912 | bytes 6815744 | tf_op jit(solution)/shard_map/output_and_grad_features/pallas_call | solution.py:312
  164.1 8.7 %collective-permute-done.25.refs_13_ = bf16[768,512]{1,0:T(8,128)(2,1)} collective-permute-done((bf16[768,512]{1,0:T(8,128)(2,1)}, bf16[768,512]{1,0:T(8,128)(2,1)}, u32[]{:S(2)}, u32[]{:S(2)}) %collective-permute-start.25) | collective-permute-done | bytes 786464 | tf_op jit(solution)/shard_map/ppermute | solution.py:33
  175.7 7.6 %weights_second.1 = (bf16[2,256,256]{2,1,0:T(8,128)(2,1)}, bf16[7,2,256,256]{3,2,1,0:T(8,128)(2,1)}, bf16[512]{0:T(512)(128)(2,1)}) custom-call(s32[7]{0:T(128)} %refs_0_.3, bf16[512,512]{1,0:T(8,128)(2,1)} %get-tuple-element.108.hidden.refs_4_.refs_1_, bf16[768,512]{1,0:T(8,128)(2,1)} %get-tuple-element.134.refs_2_, ...), custom_call_target="tpu_custom_call" | custom-call | flops 2147483648 | bytes 17302528 | tf_op jit(solution)/shard_map/weights_second/pallas_call | solution.py:312
  (87 shorter events, 22.1 us)
Async XLA Ops:
  7.2 48.2 %copy-start.8 = (bf16[256,512]{1,0:T(8,128)(2,1)S(1)}, bf16[256,512]{1,0:T(8,128)(2,1)}, u32[]{:S(2)}) copy-start(bf16[256,512]{1,0:T(8,128)(2,1)} %refs_4_.1) | copy-start | bytes 786436
  7.2 117.9 %all-gather.2.cloned.1.call-start = ((), (), s32[]{:S(2)}) async-start(), calls=%async_computation | async-start | bytes 4718592 | tf_op jit(solution)/shard_map/all_gather | solution.py:411
  7.2 12.7 %collective-permute-start = (bf16[256,512]{1,0:T(8,128)(2,1)}, bf16[256,512]{1,0:T(8,128)(2,1)S(1)}, u32[]{:S(2)}, u32[]{:S(2)}) collective-permute-start(bf16[256,512]{1,0:T(8,128)(2,1)} %refs_1_.1), channel_id=1, source_target_pairs={{0,64},{1,65},{2,66},{3,67},{4,68},{5,69},{6,70},{7,71},{8,72},{9,... | collective-permute-start | bytes 786440 | tf_op jit(solution)/shard_map/ppermute | solution.py:58
  9.8 10.2 %collective-permute-start.1 = (bf16[256,512]{1,0:T(8,128)(2,1)}, bf16[256,512]{1,0:T(8,128)(2,1)S(1)}, u32[]{:S(2)}, u32[]{:S(2)}) collective-permute-start(bf16[256,512]{1,0:T(8,128)(2,1)} %refs_1_.1), channel_id=1, source_target_pairs={{0,200},{1,201},{2,202},{3,203},{4,204},{5,205},{6,206},{7,207},{8... | collective-permute-start | bytes 786440 | tf_op jit(solution)/shard_map/ppermute | solution.py:58
  20.0 10.3 %collective-permute-start.2 = (bf16[512,512]{1,0:T(8,128)(2,1)}, bf16[512,512]{1,0:T(8,128)(2,1)S(1)}, u32[]{:S(2)}, u32[]{:S(2)}) collective-permute-start(bf16[512,512]{1,0:T(8,128)(2,1)} %get-tuple-element.92), channel_id=1, source_target_pairs={{0,1},{1,0},{2,3},{3,2},{4,5},{5,4},{6,7},{7,6},{8,9},{9,8},{10,11... | collective-permute-start | bytes 1572872 | tf_op jit(solution)/shard_map/ppermute | solution.py:33
  21.3 13.7 %collective-permute-start.3 = (bf16[512,512]{1,0:T(8,128)(2,1)}, bf16[512,512]{1,0:T(8,128)(2,1)S(1)}, u32[]{:S(2)}, u32[]{:S(2)}) collective-permute-start(bf16[512,512]{1,0:T(8,128)(2,1)} %get-tuple-element.93), channel_id=1, source_target_pairs={{0,2},{1,3},{2,0},{3,1},{4,6},{5,7},{6,4},{7,5},{8,10},{9,11},{10,... | collective-permute-start | bytes 1572872 | tf_op jit(solution)/shard_map/ppermute | solution.py:33
  22.5 25.9 %collective-permute-start.4 = (bf16[512,512]{1,0:T(8,128)(2,1)}, bf16[512,512]{1,0:T(8,128)(2,1)S(1)}, u32[]{:S(2)}, u32[]{:S(2)}) collective-permute-start(bf16[512,512]{1,0:T(8,128)(2,1)} %get-tuple-element.94), channel_id=1, source_target_pairs={{0,4},{1,5},{2,6},{3,7},{4,0},{5,1},{6,2},{7,3},{8,12},{9,13},{10,... | collective-permute-start | bytes 1572872 | tf_op jit(solution)/shard_map/ppermute | solution.py:33
  24.9 23.5 %collective-permute-start.5 = (bf16[512,512]{1,0:T(8,128)(2,1)}, bf16[512,512]{1,0:T(8,128)(2,1)S(1)}, u32[]{:S(2)}, u32[]{:S(2)}) collective-permute-start(bf16[512,512]{1,0:T(8,128)(2,1)} %get-tuple-element.95), channel_id=1, source_target_pairs={{0,8},{1,9},{2,10},{3,11},{4,12},{5,13},{6,14},{7,15},{8,0},{9,1},... | collective-permute-start | bytes 1572872 | tf_op jit(solution)/shard_map/ppermute | solution.py:33
  29.0 19.5 %collective-permute-start.6 = (bf16[512,512]{1,0:T(8,128)(2,1)}, bf16[512,512]{1,0:T(8,128)(2,1)S(1)}, u32[]{:S(2)}, u32[]{:S(2)}) collective-permute-start(bf16[512,512]{1,0:T(8,128)(2,1)} %get-tuple-element.96), channel_id=1, source_target_pairs={{0,16},{1,17},{2,18},{3,19},{4,20},{5,21},{6,22},{7,23},{8,24},{9,... | collective-permute-start | bytes 1572872 | tf_op jit(solution)/shard_map/ppermute | solution.py:33
  30.3 25.1 %collective-permute-start.7 = (bf16[512,512]{1,0:T(8,128)(2,1)}, bf16[512,512]{1,0:T(8,128)(2,1)S(1)}, u32[]{:S(2)}, u32[]{:S(2)}) collective-permute-start(bf16[512,512]{1,0:T(8,128)(2,1)} %get-tuple-element.97), channel_id=1, source_target_pairs={{0,32},{1,33},{2,34},{3,35},{4,36},{5,37},{6,38},{7,39},{8,40},{9,... | collective-permute-start | bytes 1572872 | tf_op jit(solution)/shard_map/ppermute | solution.py:33
  56.5 13.0 %collective-permute-start.8 = (bf16[512,512]{1,0:T(8,128)(2,1)}, bf16[512,512]{1,0:T(8,128)(2,1)S(1)}, u32[]{:S(2)}, u32[]{:S(2)}) collective-permute-start(bf16[512,512]{1,0:T(8,128)(2,1)} %get-tuple-element.160), channel_id=1, source_target_pairs={{0,64},{1,65},{2,66},{3,67},{4,68},{5,69},{6,70},{7,71},{8,72},{9,... | collective-permute-start | bytes 1572872 | tf_op jit(solution)/shard_map/ppermute | solution.py:58
  56.8 12.8 %collective-permute-start.9 = (bf16[512,512]{1,0:T(8,128)(2,1)}, bf16[512,512]{1,0:T(8,128)(2,1)S(1)}, u32[]{:S(2)}, u32[]{:S(2)}) collective-permute-start(bf16[512,512]{1,0:T(8,128)(2,1)} %get-tuple-element.159), channel_id=1, source_target_pairs={{0,200},{1,201},{2,202},{3,203},{4,204},{5,205},{6,206},{7,207},{8... | collective-permute-start | bytes 1572872 | tf_op jit(solution)/shard_map/ppermute | solution.py:58
  69.6 12.0 %collective-permute-start.10 = (bf16[512,512]{1,0:T(8,128)(2,1)S(1)}, bf16[512,512]{1,0:T(8,128)(2,1)S(1)}, u32[]{:S(2)}, u32[]{:S(2)}) collective-permute-start(bf16[512,512]{1,0:T(8,128)(2,1)S(1)} %collective-permute-done.8.refs_1_.refs_17_.refs_16_), channel_id=1, source_target_pairs={{0,64},{1,65},{2,66},{3,67},{4,68},{5,69},{6,70},{7,71},{8,72},{9,... | collective-permute-start | bytes 1572872 | tf_op jit(solution)/shard_map/ppermute | solution.py:58
  71.2 12.2 %collective-permute-start.11 = (bf16[512,512]{1,0:T(8,128)(2,1)S(1)}, bf16[512,512]{1,0:T(8,128)(2,1)S(1)}, u32[]{:S(2)}, u32[]{:S(2)}) collective-permute-start(bf16[512,512]{1,0:T(8,128)(2,1)S(1)} %collective-permute-done.9.refs_4_.refs_20_.refs_19_), channel_id=1, source_target_pairs={{0,200},{1,201},{2,202},{3,203},{4,204},{5,205},{6,206},{7,207},{8... | collective-permute-start | bytes 1572872 | tf_op jit(solution)/shard_map/ppermute | solution.py:58
  72.3 24.1 %collective-permute-start.12 = (bf16[512,512]{1,0:T(8,128)(2,1)}, bf16[512,512]{1,0:T(8,128)(2,1)S(1)}, u32[]{:S(2)}, u32[]{:S(2)}) collective-permute-start(bf16[512,512]{1,0:T(8,128)(2,1)} %get-tuple-element.115), channel_id=1, source_target_pairs={{0,4},{1,5},{2,6},{3,7},{4,0},{5,1},{6,2},{7,3},{8,12},{9,13},{10,... | collective-permute-start | bytes 1572872 | tf_op jit(solution)/shard_map/ppermute | solution.py:33
  72.8 23.6 %collective-permute-start.13 = (bf16[512,512]{1,0:T(8,128)(2,1)}, bf16[512,512]{1,0:T(8,128)(2,1)S(1)}, u32[]{:S(2)}, u32[]{:S(2)}) collective-permute-start(bf16[512,512]{1,0:T(8,128)(2,1)} %get-tuple-element.116), channel_id=1, source_target_pairs={{0,32},{1,33},{2,34},{3,35},{4,36},{5,37},{6,38},{7,39},{8,40},{9,... | collective-permute-start | bytes 1572872 | tf_op jit(solution)/shard_map/ppermute | solution.py:33
  75.2 24.2 %collective-permute-start.14 = (bf16[512,512]{1,0:T(8,128)(2,1)}, bf16[512,512]{1,0:T(8,128)(2,1)}, u32[]{:S(2)}, u32[]{:S(2)}) collective-permute-start(bf16[512,512]{1,0:T(8,128)(2,1)} %get-tuple-element.119), channel_id=1, source_target_pairs={{0,2},{1,3},{2,0},{3,1},{4,6},{5,7},{6,4},{7,5},{8,10},{9,11},{10,... | collective-permute-start | bytes 1572872 | tf_op jit(solution)/shard_map/ppermute | solution.py:33
  83.3 16.1 %collective-permute-start.15 = (bf16[512,512]{1,0:T(8,128)(2,1)}, bf16[512,512]{1,0:T(8,128)(2,1)}, u32[]{:S(2)}, u32[]{:S(2)}) collective-permute-start(bf16[512,512]{1,0:T(8,128)(2,1)} %get-tuple-element.120), channel_id=1, source_target_pairs={{0,16},{1,17},{2,18},{3,19},{4,20},{5,21},{6,22},{7,23},{8,24},{9,... | collective-permute-start | bytes 1572872 | tf_op jit(solution)/shard_map/ppermute | solution.py:33
  86.7 12.8 %collective-permute-start.16 = (bf16[512,512]{1,0:T(8,128)(2,1)}, bf16[512,512]{1,0:T(8,128)(2,1)}, u32[]{:S(2)}, u32[]{:S(2)}) collective-permute-start(bf16[512,512]{1,0:T(8,128)(2,1)} %get-tuple-element.121), channel_id=1, source_target_pairs={{0,1},{1,0},{2,3},{3,2},{4,5},{5,4},{6,7},{7,6},{8,9},{9,8},{10,11... | collective-permute-start | bytes 1572872 | tf_op jit(solution)/shard_map/ppermute | solution.py:33
  96.5 21.1 %collective-permute-start.17 = (bf16[768,512]{1,0:T(8,128)(2,1)}, bf16[768,512]{1,0:T(8,128)(2,1)S(1)}, u32[]{:S(2)}, u32[]{:S(2)}) collective-permute-start(bf16[768,512]{1,0:T(8,128)(2,1)} %feature_rows.1.refs_2_), channel_id=1, source_target_pairs={{0,4},{1,5},{2,6},{3,7},{4,0},{5,1},{6,2},{7,3},{8,12},{9,13},{10,... | collective-permute-start | bytes 2359304 | tf_op jit(solution)/shard_map/ppermute | solution.py:33
  96.6 21.5 %collective-permute-start.18 = (bf16[768,512]{1,0:T(8,128)(2,1)}, bf16[768,512]{1,0:T(8,128)(2,1)}, u32[]{:S(2)}, u32[]{:S(2)}) collective-permute-start(bf16[768,512]{1,0:T(8,128)(2,1)} %feature_rows.1.refs_2_), channel_id=1, source_target_pairs={{0,32},{1,33},{2,34},{3,35},{4,36},{5,37},{6,38},{7,39},{8,40},{9,... | collective-permute-start | bytes 2359304 | tf_op jit(solution)/shard_map/ppermute | solution.py:33
  99.5 31.4 %collective-permute-start.19 = (bf16[768,512]{1,0:T(8,128)(2,1)}, bf16[768,512]{1,0:T(8,128)(2,1)}, u32[]{:S(2)}, u32[]{:S(2)}) collective-permute-start(bf16[768,512]{1,0:T(8,128)(2,1)} %feature_rows.1.refs_2_), channel_id=1, source_target_pairs={{0,2},{1,3},{2,0},{3,1},{4,6},{5,7},{6,4},{7,5},{8,10},{9,11},{10,... | collective-permute-start | bytes 2359304 | tf_op jit(solution)/shard_map/ppermute | solution.py:33
  99.6 35.0 %collective-permute-start.20 = (bf16[768,512]{1,0:T(8,128)(2,1)}, bf16[768,512]{1,0:T(8,128)(2,1)}, u32[]{:S(2)}, u32[]{:S(2)}) collective-permute-start(bf16[768,512]{1,0:T(8,128)(2,1)} %feature_rows.1.refs_2_), channel_id=1, source_target_pairs={{0,16},{1,17},{2,18},{3,19},{4,20},{5,21},{6,22},{7,23},{8,24},{9,... | collective-permute-start | bytes 2359304 | tf_op jit(solution)/shard_map/ppermute | solution.py:33
  99.7 34.9 %collective-permute-start.21 = (bf16[768,512]{1,0:T(8,128)(2,1)}, bf16[768,512]{1,0:T(8,128)(2,1)}, u32[]{:S(2)}, u32[]{:S(2)}) collective-permute-start(bf16[768,512]{1,0:T(8,128)(2,1)} %feature_rows.1.refs_2_), channel_id=1, source_target_pairs={{0,1},{1,0},{2,3},{3,2},{4,5},{5,4},{6,7},{7,6},{8,9},{9,8},{10,11... | collective-permute-start | bytes 2359304 | tf_op jit(solution)/shard_map/ppermute | solution.py:33
  134.6 5.3 %collective-permute-start.22 = (bf16[768,512]{1,0:T(8,128)(2,1)}, bf16[768,512]{1,0:T(8,128)(2,1)S(1)}, u32[]{:S(2)}, u32[]{:S(2)}) collective-permute-start(bf16[768,512]{1,0:T(8,128)(2,1)} %get-tuple-element.134.refs_2_), channel_id=1, source_target_pairs={{0,1},{1,0},{2,3},{3,2},{4,5},{5,4},{6,7},{7,6},{8,9},{9,8},{10,11... | collective-permute-start | bytes 2359304 | tf_op jit(solution)/shard_map/ppermute | solution.py:33
  135.4 19.5 %collective-permute-start.24 = (bf16[768,512]{1,0:T(8,128)(2,1)}, bf16[768,512]{1,0:T(8,128)(2,1)S(1)}, u32[]{:S(2)}, u32[]{:S(2)}) collective-permute-start(bf16[768,512]{1,0:T(8,128)(2,1)} %get-tuple-element.134.refs_2_), channel_id=1, source_target_pairs={{0,2},{1,3},{2,0},{3,1},{4,6},{5,7},{6,4},{7,5},{8,10},{9,11},{10,... | collective-permute-start | bytes 2359304 | tf_op jit(solution)/shard_map/ppermute | solution.py:33
  135.4 28.7 %collective-permute-start.26 = (bf16[768,512]{1,0:T(8,128)(2,1)}, bf16[768,512]{1,0:T(8,128)(2,1)S(1)}, u32[]{:S(2)}, u32[]{:S(2)}) collective-permute-start(bf16[768,512]{1,0:T(8,128)(2,1)} %get-tuple-element.134.refs_2_), channel_id=1, source_target_pairs={{0,16},{1,17},{2,18},{3,19},{4,20},{5,21},{6,22},{7,23},{8,24},{9,... | collective-permute-start | bytes 2359304 | tf_op jit(solution)/shard_map/ppermute | solution.py:33
  136.6 36.2 %collective-permute-start.25 = (bf16[768,512]{1,0:T(8,128)(2,1)}, bf16[768,512]{1,0:T(8,128)(2,1)}, u32[]{:S(2)}, u32[]{:S(2)}) collective-permute-start(bf16[768,512]{1,0:T(8,128)(2,1)} %get-tuple-element.134.refs_2_), channel_id=1, source_target_pairs={{0,4},{1,5},{2,6},{3,7},{4,0},{5,1},{6,2},{7,3},{8,12},{9,13},{10,... | collective-permute-start | bytes 2359304 | tf_op jit(solution)/shard_map/ppermute | solution.py:33
  139.5 34.8 %collective-permute-start.27 = (bf16[768,512]{1,0:T(8,128)(2,1)}, bf16[768,512]{1,0:T(8,128)(2,1)}, u32[]{:S(2)}, u32[]{:S(2)}) collective-permute-start(bf16[768,512]{1,0:T(8,128)(2,1)} %get-tuple-element.134.refs_2_), channel_id=1, source_target_pairs={{0,32},{1,33},{2,34},{3,35},{4,36},{5,37},{6,38},{7,39},{8,40},{9,... | collective-permute-start | bytes 2359304 | tf_op jit(solution)/shard_map/ppermute | solution.py:33
  139.9 18.0 %collective-permute-start.23 = (bf16[256,512]{1,0:T(8,128)(2,1)}, bf16[256,512]{1,0:T(8,128)(2,1)}, u32[]{:S(2)}, u32[]{:S(2)}) collective-permute-start(bf16[256,512]{1,0:T(8,128)(2,1)} %get-tuple-element.135), channel_id=1, source_target_pairs={{0,8},{1,9},{2,10},{3,11},{4,12},{5,13},{6,14},{7,15},{8,0},{9,1},... | collective-permute-start | bytes 786440 | tf_op jit(solution)/shard_map/ppermute | solution.py:33
  154.9 19.3 %collective-permute-start.28 = (bf16[256,512]{1,0:T(8,128)(2,1)}, bf16[256,512]{1,0:T(8,128)(2,1)S(1)}, u32[]{:S(2)}, u32[]{:S(2)}) collective-permute-start(bf16[256,512]{1,0:T(8,128)(2,1)} %slice.6), channel_id=1, source_target_pairs={{0,64},{1,65},{2,66},{3,67},{4,68},{5,69},{6,70},{7,71},{8,72},{9,... | collective-permute-start | bytes 786440 | tf_op jit(solution)/shard_map/ppermute | solution.py:58
  157.8 16.4 %collective-permute-start.29 = (bf16[256,512]{1,0:T(8,128)(2,1)S(1)}, bf16[256,512]{1,0:T(8,128)(2,1)S(1)}, u32[]{:S(2)}, u32[]{:S(2)}) collective-permute-start(bf16[256,512]{1,0:T(8,128)(2,1)S(1)} %slice.7), channel_id=1, source_target_pairs={{0,200},{1,201},{2,202},{3,203},{4,204},{5,205},{6,206},{7,207},{8... | collective-permute-start | bytes 786440 | tf_op jit(solution)/shard_map/ppermute | solution.py:58
  (22 other events, 446.8 us)
Sparse Core Ops, SparseCore 0:
  69.7 55.3 all-gather.1

commit v3 on v2

--- a/solution.py
+++ b/solution.py
@@ -387,9 +387,7 @@
     up, down, *tied = after(*ends[:2], *[got[bit] for bit in bits])
     got = dict(zip(bits, tied))
     features_z[0] = (up, down)
-    features_z.append(
-        both_ways(*[jnp.concatenate([value, grad_out], axis=0) for value in (up, down)])
-    )
+    features_z.append(both_ways(up, down))
     late, local_first, *sent = call(
         middle_kernel,
         "hidden_and_grad_pre",
@@ -409,7 +407,9 @@
     up, down, late = after(*features_z[1], late)
     features_z[1] = (up, down)
     gathered = lax.all_gather(late, ("z_hi", "dp"), axis=0, tiled=True)
-    features_z.append(both_ways(up, down))
+    features_z.append(
+        both_ways(*[jnp.concatenate([value, grad_out], axis=0) for value in (up, down)])
+    )
     got_late = send({bit: sent[bit] for bit in (X2, Y2, X1)})
     features_z[2], (sent[Y1], sent[CORE]) = tie(features_z[2], sent[Y1], sent[CORE])
     got_late.update(send({Y1: sent[Y1], CORE: sent[CORE]}))
@@ -452,7 +452,8 @@
         ),
     )
     up, down, bias_grad = after(*[value[ROWS:] for value in features_z[2]], bias_grad)
-    grad_z = [*features_z[1:], both_ways(up, down)]
+    grad_z = [features_z[2], both_ways(up, down)]
+    grad_z.append(both_ways(*grad_z[1]))
     output, grad_in = call(
         last_kernel,
         "output_and_grad_features",

time: 190 us -> 198 us (1.042)
  waiting for transfers between devices: 80.1 us -> 87 us
    ppermute x8 -> x10, waiting for transfers between devices: 13.7 us -> 25.9 us  [along_z(): return lax.ppermute(value, ('dp', *FEAT), pairs)]
    ppermute x22, waiting for transfers between devices: 59.4 us -> 54.4 us  [from_partner(): return lax.ppermute(value, FEAT, pairs)]
    ppermute x8 -> x10, starting transfers between devices: 14.6 us -> 18.1 us  [along_z(): return lax.ppermute(value, ('dp', *FEAT), pairs)]
    ppermute x22, starting transfers between devices: 41.7 us -> 39.5 us  [from_partner(): return lax.ppermute(value, FEAT, pairs)]
  transfers between devices with their start and end apart: 31 -> 33, of which waited for: 16 -> 15; matrix products, arithmetic and copies ran while one was open for 0% -> 0% of each run, Pallas kernels for 15% -> 14%
where the time goes in v3:
time: 198 us; the launch traced here: 197 us
  waiting for transfers between devices  87 us (44%)
  starting transfers between devices  57.7 us (29%)
  Pallas kernels  36.1 us (18%)
  between operations  14.4 us (7%)
    ppermute x22, waiting for transfers between devices, from_partner(): return lax.ppermute(value, FEAT, pairs)  54.4 us
    ppermute x22, starting transfers between devices, from_partner(): return lax.ppermute(value, FEAT, pairs)  39.5 us
    pallas_call x7, Pallas kernels, call(): pl.pallas_call(kernel, grid=(1,), out_shape=out_shape, in_specs=[SCALARS]...  36.1 us
    ppermute x10, waiting for transfers between devices, along_z(): return lax.ppermute(value, ('dp', *FEAT), pairs)  25.9 us
    ppermute x10, starting transfers between devices, along_z(): return lax.ppermute(value, ('dp', *FEAT), pairs)  18.1 us
    all_gather x1, waiting for transfers between devices, on_device(): gathered = lax.all_gather(late, ('z_hi', 'dp'), axis=0, tiled=True)  6.68 us
  transfers between devices with their start and end apart: 33, of which 15 were waited for; matrix products, arithmetic and copies ran while one was open for 0% of the time, Pallas kernels for 14%

profile of v3, /device:TPU:1, one launch (start us, length us, event | category | flops | bytes accessed | tf_op | source)
XLA Modules:
  0.0 197.0 jit_solution(4577133333629869983)
XLA Ops:
  7.2 2.5 %collective-permute-start = (bf16[256,512]{1,0:T(8,128)(2,1)}, bf16[256,512]{1,0:T(8,128)(2,1)}, u32[]{:S(2)}, u32[]{:S(2)}) collective-permute-start(bf16[256,512]{1,0:T(8,128)(2,1)} %refs_1_.1), channel_id=1, source_target_pairs={{0,64},{1,65},{2,66},{3,67},{4,68},{5,69},{6,70},{7,71},{8,72},{9,... | collective-permute-start | bytes 786440 | tf_op jit(solution)/shard_map/ppermute | solution.py:58
  9.8 4.0 %collective-permute-start.1 = (bf16[256,512]{1,0:T(8,128)(2,1)}, bf16[256,512]{1,0:T(8,128)(2,1)S(1)}, u32[]{:S(2)}, u32[]{:S(2)}) collective-permute-start(bf16[256,512]{1,0:T(8,128)(2,1)} %refs_1_.1), channel_id=1, source_target_pairs={{0,200},{1,201},{2,202},{3,203},{4,204},{5,205},{6,206},{7,207},{8... | collective-permute-start | bytes 786440 | tf_op jit(solution)/shard_map/ppermute | solution.py:58
  13.8 4.2 %products_second.1 = (f32[256,512]{1,0:T(8,128)}, bf16[512,512]{1,0:T(8,128)(2,1)}, bf16[512,512]{1,0:T(8,128)(2,1)}, bf16[512,512]{1,0:T(8,128)(2,1)}, bf16[512...) custom-call(s32[7]{0:T(128)} %refs_0_.3, bf16[256,512]{1,0:T(8,128)(2,1)} %refs_1_.1, ...), custom_call_target="tpu_custom_call" | custom-call | flops 536870912 | bytes 6291456 | tf_op jit(solution)/shard_map/products_second/pallas_call | solution.py:312
  18.0 2.0 %collective-permute-done.refs_0_.refs_16_ = bf16[256,512]{1,0:T(8,128)(2,1)} collective-permute-done((bf16[256,512]{1,0:T(8,128)(2,1)}, bf16[256,512]{1,0:T(8,128)(2,1)}, u32[]{:S(2)}, u32[]{:S(2)}) %collective-permute-start) | collective-permute-done | bytes 262176 | tf_op jit(solution)/shard_map/ppermute | solution.py:58
  23.2 2.5 %collective-permute-start.4 = (bf16[512,512]{1,0:T(8,128)(2,1)}, bf16[512,512]{1,0:T(8,128)(2,1)S(1)}, u32[]{:S(2)}, u32[]{:S(2)}) collective-permute-start(bf16[512,512]{1,0:T(8,128)(2,1)} %get-tuple-element.94), channel_id=1, source_target_pairs={{0,4},{1,5},{2,6},{3,7},{4,0},{5,1},{6,2},{7,3},{8,12},{9,13},{10,... | collective-permute-start | bytes 1572872 | tf_op jit(solution)/shard_map/ppermute | solution.py:33
  25.6 4.0 %collective-permute-start.5 = (bf16[512,512]{1,0:T(8,128)(2,1)}, bf16[512,512]{1,0:T(8,128)(2,1)S(1)}, u32[]{:S(2)}, u32[]{:S(2)}) collective-permute-start(bf16[512,512]{1,0:T(8,128)(2,1)} %get-tuple-element.95), channel_id=1, source_target_pairs={{0,8},{1,9},{2,10},{3,11},{4,12},{5,13},{6,14},{7,15},{8,0},{9,1},... | collective-permute-start | bytes 1572872 | tf_op jit(solution)/shard_map/ppermute | solution.py:33
  30.9 2.6 %collective-permute-start.7 = (bf16[512,512]{1,0:T(8,128)(2,1)}, bf16[512,512]{1,0:T(8,128)(2,1)S(1)}, u32[]{:S(2)}, u32[]{:S(2)}) collective-permute-start(bf16[512,512]{1,0:T(8,128)(2,1)} %get-tuple-element.97), channel_id=1, source_target_pairs={{0,32},{1,33},{2,34},{3,35},{4,36},{5,37},{6,38},{7,39},{8,40},{9,... | collective-permute-start | bytes 1572872 | tf_op jit(solution)/shard_map/ppermute | solution.py:33
  33.6 2.2 %collective-permute-done.3.refs_1_.refs_7_ = bf16[512,512]{1,0:T(8,128)(2,1)S(1)} collective-permute-done((bf16[512,512]{1,0:T(8,128)(2,1)}, bf16[512,512]{1,0:T(8,128)(2,1)S(1)}, u32[]{:S(2)}, u32[]{:S(2)}) %collective-permute-start.3) | collective-permute-done | bytes 524320 | tf_op jit(solution)/shard_map/ppermute | solution.py:33
  35.8 13.4 %collective-permute-done.4.refs_2_.refs_8_ = bf16[512,512]{1,0:T(8,128)(2,1)S(1)} collective-permute-done((bf16[512,512]{1,0:T(8,128)(2,1)}, bf16[512,512]{1,0:T(8,128)(2,1)S(1)}, u32[]{:S(2)}, u32[]{:S(2)}) %collective-permute-start.4) | collective-permute-done | bytes 524320 | tf_op jit(solution)/shard_map/ppermute | solution.py:33
  49.2 6.9 %collective-permute-done.7.refs_5_.refs_10_ = bf16[512,512]{1,0:T(8,128)(2,1)S(1)} collective-permute-done((bf16[512,512]{1,0:T(8,128)(2,1)}, bf16[512,512]{1,0:T(8,128)(2,1)S(1)}, u32[]{:S(2)}, u32[]{:S(2)}) %collective-permute-start.7) | collective-permute-done | bytes 524320 | tf_op jit(solution)/shard_map/ppermute | solution.py:33
  56.3 2.5 %collective-permute-start.9 = (bf16[256,512]{1,0:T(8,128)(2,1)}, bf16[256,512]{1,0:T(8,128)(2,1)S(1)}, u32[]{:S(2)}, u32[]{:S(2)}) collective-permute-start(bf16[256,512]{1,0:T(8,128)(2,1)} %copy-done.16), channel_id=1, source_target_pairs={{0,200},{1,201},{2,202},{3,203},{4,204},{5,205},{6,206},{7,207},{8... | collective-permute-start | bytes 786440 | tf_op jit(solution)/shard_map/ppermute | solution.py:58
  58.9 6.4 %hidden_and_grad_pre.1 = (bf16[512,512]{1,0:T(8,128)(2,1)}, f32[256,512]{1,0:T(8,128)}, bf16[512,512]{1,0:T(8,128)(2,1)}, bf16[512,512]{1,0:T(8,128)(2,1)}, bf16...) custom-call(s32[7]{0:T(128)} %refs_0_.3, ...), custom_call_target="tpu_custom_call" | custom-call | flops 1073741824 | bytes 9962496 | tf_op jit(solution)/shard_map/hidden_and_grad_pre/pallas_call | solution.py:312
  65.5 2.7 %collective-permute-start.11 = (bf16[512,512]{1,0:T(8,128)(2,1)S(1)}, bf16[512,512]{1,0:T(8,128)(2,1)S(1)}, u32[]{:S(2)}, u32[]{:S(2)}) collective-permute-start(bf16[512,512]{1,0:T(8,128)(2,1)S(1)} %get-tuple-element.159), channel_id=1, source_target_pairs={{0,200},{1,201},{2,202},{3,203},{4,204},{5,205},{6,206},{7,207},{8... | collective-permute-start | bytes 1572872 | tf_op jit(solution)/shard_map/ppermute | solution.py:58
  69.4 8.4 %collective-permute-done.10.refs_2_.refs_18_.refs_16_ = bf16[512,512]{1,0:T(8,128)(2,1)S(1)} collective-permute-done((bf16[512,512]{1,0:T(8,128)(2,1)S(1)}, bf16[512,512]{1,0:T(8,128)(2,1)S(1)}, u32[]{:S(2)}, u32[]{:S(2)}) %collective-permute-start.10) | collective-permute-done | bytes 524320 | tf_op jit(solution)/shard_map/ppermute | solution.py:58
  77.8 1.9 collective-permute-done.11.refs_5_.refs_21_.refs_19_
  80.6 8.8 %collective-permute-start.16 = (bf16[512,512]{1,0:T(8,128)(2,1)}, bf16[512,512]{1,0:T(8,128)(2,1)}, u32[]{:S(2)}, u32[]{:S(2)}) collective-permute-start(bf16[512,512]{1,0:T(8,128)(2,1)} %get-tuple-element.121), channel_id=1, source_target_pairs={{0,1},{1,0},{2,3},{3,2},{4,5},{5,4},{6,7},{7,6},{8,9},{9,8},{10,11... | collective-permute-start | bytes 1572872 | tf_op jit(solution)/shard_map/ppermute | solution.py:33
  89.4 2.7 %feature_rows.1.refs_2_ = bf16[768,512]{1,0:T(8,128)(2,1)} custom-call(s32[7]{0:T(128)} %refs_0_.3, bf16[256,512]{1,0:T(8,128)(2,1)} %collective-permute-done.refs_0_.refs_16_, bf16[256,512]{1,0:T(8,128)(2,1)} %copy-done.4, bf16[512,512]{1,0:T(8,128)(2,1)} %copy-done, bf16[256,512]{1,0:T(8,128)(2,1)} %copy-done.16, bf16[256,512]{1,0:T(8,128)(2,1)} %copy-done.5, ...), custom_call_target="tpu_custom_call" | custom-call | bytes 2883584 | tf_op jit(solution)/shard_map/feature_rows/pallas_call | solution.py:312
  94.4 7.4 %collective-permute-start.21 = (bf16[768,512]{1,0:T(8,128)(2,1)}, bf16[768,512]{1,0:T(8,128)(2,1)}, u32[]{:S(2)}, u32[]{:S(2)}) collective-permute-start(bf16[768,512]{1,0:T(8,128)(2,1)} %feature_rows.1.refs_2_), channel_id=1, source_target_pairs={{0,1},{1,0},{2,3},{3,2},{4,5},{5,4},{6,7},{7,6},{8,9},{9,8},{10,11... | collective-permute-start | bytes 2359304 | tf_op jit(solution)/shard_map/ppermute | solution.py:33
  101.8 10.6 %collective-permute-done.17.refs_13_ = bf16[768,512]{1,0:T(8,128)(2,1)S(1)} collective-permute-done((bf16[768,512]{1,0:T(8,128)(2,1)}, bf16[768,512]{1,0:T(8,128)(2,1)S(1)}, u32[]{:S(2)}, u32[]{:S(2)}) %collective-permute-start.17) | collective-permute-done | bytes 786464 | tf_op jit(solution)/shard_map/ppermute | solution.py:33
  113.8 6.7 %all-gather.2.cloned.1.call-done.gathered.refs_5_ = bf16[4096,512]{1,0:T(8,128)(2,1)} async-done(((bf16[512,512]{1,0:T(8,128)(2,1)}), bf16[4096,512]{1,0:T(8,128)(2,1)}) %all-gather.2.cloned.1.call-update) | async-done | bytes 4194320 | tf_op jit(solution)/shard_map/all_gather | solution.py:409
  120.5 2.9 %hidden_rows.1 = (bf16[768,512]{1,0:T(8,128)(2,1)}, bf16[256,512]{1,0:T(8,128)(2,1)}) custom-call(s32[7]{0:T(128)} %refs_0_.3, bf16[4096,512]{1,0:T(8,128)(2,1)} %all-gather.2.cloned.1.call-done.gathered.refs_5_), custom_call_target="tpu_custom_call" | custom-call | bytes 5242880 | tf_op jit(solution)/shard_map/hidden_rows/pallas_call | solution.py:312
  123.4 2.6 %collective-permute-done.19.refs_12_ = bf16[768,512]{1,0:T(8,128)(2,1)} collective-permute-done((bf16[768,512]{1,0:T(8,128)(2,1)}, bf16[768,512]{1,0:T(8,128)(2,1)}, u32[]{:S(2)}, u32[]{:S(2)}) %collective-permute-start.19) | collective-permute-done | bytes 786464 | tf_op jit(solution)/shard_map/ppermute | solution.py:33
  126.0 3.5 %collective-permute-done.20.refs_14_ = bf16[768,512]{1,0:T(8,128)(2,1)} collective-permute-done((bf16[768,512]{1,0:T(8,128)(2,1)}, bf16[768,512]{1,0:T(8,128)(2,1)}, u32[]{:S(2)}, u32[]{:S(2)}) %collective-permute-start.20) | collective-permute-done | bytes 786464 | tf_op jit(solution)/shard_map/ppermute | solution.py:33
  129.5 3.2 %collective-permute-start.22 = (bf16[768,512]{1,0:T(8,128)(2,1)}, bf16[768,512]{1,0:T(8,128)(2,1)S(1)}, u32[]{:S(2)}, u32[]{:S(2)}) collective-permute-start(bf16[768,512]{1,0:T(8,128)(2,1)} %get-tuple-element.134.refs_2_), channel_id=1, source_target_pairs={{0,1},{1,0},{2,3},{3,2},{4,5},{5,4},{6,7},{7,6},{8,9},{9,8},{10,11... | collective-permute-start | bytes 2359304 | tf_op jit(solution)/shard_map/ppermute | solution.py:33
  132.7 7.7 %weights_first.1 = (bf16[2,256,256]{2,1,0:T(8,128)(2,1)}, bf16[7,2,256,256]{3,2,1,0:T(8,128)(2,1)}, bf16[512]{0:T(512)(128)(2,1)}) custom-call(s32[7]{0:T(128)} %refs_0_.3, bf16[256,512]{1,0:T(8,128)(2,1)} %refs_1_.1, bf16[768,512]{1,0:T(8,128)(2,1)} %feature_rows.1.refs_2_, bf16[512,512]{1,0:T(8,128)(2,1)} %copy-done.13, ...), custom_call_target="tpu_custom_call" | custom-call | flops 2147483648 | bytes 17040384 | tf_op jit(solution)/shard_map/weights_first/pallas_call | solution.py:312
  140.8 2.0 %collective-permute-start.25 = (bf16[768,512]{1,0:T(8,128)(2,1)S(1)}, bf16[768,512]{1,0:T(8,128)(2,1)}, u32[]{:S(2)}, u32[]{:S(2)}) collective-permute-start(bf16[768,512]{1,0:T(8,128)(2,1)S(1)} %copy-done.17), channel_id=1, source_target_pairs={{0,4},{1,5},{2,6},{3,7},{4,0},{5,1},{6,2},{7,3},{8,12},{9,13},{10,... | collective-permute-start | bytes 2359304 | tf_op jit(solution)/shard_map/ppermute | solution.py:33
  142.8 7.8 %collective-permute-done.28.refs_17_ = bf16[256,512]{1,0:T(8,128)(2,1)S(1)} collective-permute-done((bf16[256,512]{1,0:T(8,128)(2,1)S(1)}, bf16[256,512]{1,0:T(8,128)(2,1)S(1)}, u32[]{:S(2)}, u32[]{:S(2)}) %collective-permute-start.28) | collective-permute-done | bytes 262176 | tf_op jit(solution)/shard_map/ppermute | solution.py:58
  152.6 5.7 %collective-permute-done.30.refs_20_ = bf16[256,512]{1,0:T(8,128)(2,1)S(1)} collective-permute-done((bf16[256,512]{1,0:T(8,128)(2,1)S(1)}, bf16[256,512]{1,0:T(8,128)(2,1)S(1)}, u32[]{:S(2)}, u32[]{:S(2)}) %collective-permute-start.30) | collective-permute-done | bytes 262176 | tf_op jit(solution)/shard_map/ppermute | solution.py:58
  159.9 12.3 %collective-permute-done.23.refs_5_ = bf16[256,512]{1,0:T(8,128)(2,1)} collective-permute-done((bf16[256,512]{1,0:T(8,128)(2,1)}, bf16[256,512]{1,0:T(8,128)(2,1)}, u32[]{:S(2)}, u32[]{:S(2)}) %collective-permute-start.23) | collective-permute-done | bytes 262176 | tf_op jit(solution)/shard_map/ppermute | solution.py:33
  172.2 4.8 %collective-permute-start.31 = (bf16[256,512]{1,0:T(8,128)(2,1)S(1)}, bf16[256,512]{1,0:T(8,128)(2,1)}, u32[]{:S(2)}, u32[]{:S(2)}) collective-permute-start(bf16[256,512]{1,0:T(8,128)(2,1)S(1)} %collective-permute-done.30.refs_20_), channel_id=1, source_target_pairs={{0,200},{1,201},{2,202},{3,203},{4,204},{5,205},{6,206},{7,207},{8... | collective-permute-start | bytes 786440 | tf_op jit(solution)/shard_map/ppermute | solution.py:58
  177.0 4.6 %output_and_grad_features.1 = (bf16[256,512]{1,0:T(8,128)(2,1)}, bf16[256,512]{1,0:T(8,128)(2,1)}) custom-call(s32[7]{0:T(128)} %refs_0_.3, bf16[512,512]{1,0:T(8,128)(2,1)} %get-tuple-element.108.hidden.refs_4_.refs_1_, bf16[512,512]{1,0:T(8,128)(2,1)} %collective-permute-done.16.refs_0_.refs_6_, bf16[512,512]{1,0:T(8,128)(2,1)} %copy-done.9, ...), custom_call_target="tpu_custom_call" | custom-call | flops 536870912 | bytes 6815744 | tf_op jit(solution)/shard_map/output_and_grad_features/pallas_call | solution.py:312
  182.6 7.6 %weights_second.1 = (bf16[2,256,256]{2,1,0:T(8,128)(2,1)}, bf16[7,2,256,256]{3,2,1,0:T(8,128)(2,1)}, bf16[512]{0:T(512)(128)(2,1)}) custom-call(s32[7]{0:T(128)} %refs_0_.3, bf16[512,512]{1,0:T(8,128)(2,1)} %get-tuple-element.108.hidden.refs_4_.refs_1_, bf16[768,512]{1,0:T(8,128)(2,1)} %get-tuple-element.134.refs_2_, ...), custom_call_target="tpu_custom_call" | custom-call | flops 2147483648 | bytes 16778240 | tf_op jit(solution)/shard_map/weights_second/pallas_call | solution.py:312
  (97 shorter events, 15.4 us)
Async XLA Ops:
  7.2 113.3 %all-gather.2.cloned.1.call-start = ((), (), s32[]{:S(2)}) async-start(), calls=%async_computation | async-start | bytes 4718592 | tf_op jit(solution)/shard_map/all_gather | solution.py:409
  7.2 12.8 %collective-permute-start = (bf16[256,512]{1,0:T(8,128)(2,1)}, bf16[256,512]{1,0:T(8,128)(2,1)}, u32[]{:S(2)}, u32[]{:S(2)}) collective-permute-start(bf16[256,512]{1,0:T(8,128)(2,1)} %refs_1_.1), channel_id=1, source_target_pairs={{0,64},{1,65},{2,66},{3,67},{4,68},{5,69},{6,70},{7,71},{8,72},{9,... | collective-permute-start | bytes 786440 | tf_op jit(solution)/shard_map/ppermute | solution.py:58
  9.8 10.3 %collective-permute-start.1 = (bf16[256,512]{1,0:T(8,128)(2,1)}, bf16[256,512]{1,0:T(8,128)(2,1)S(1)}, u32[]{:S(2)}, u32[]{:S(2)}) collective-permute-start(bf16[256,512]{1,0:T(8,128)(2,1)} %refs_1_.1), channel_id=1, source_target_pairs={{0,200},{1,201},{2,202},{3,203},{4,204},{5,205},{6,206},{7,207},{8... | collective-permute-start | bytes 786440 | tf_op jit(solution)/shard_map/ppermute | solution.py:58
  20.8 10.2 %collective-permute-start.2 = (bf16[512,512]{1,0:T(8,128)(2,1)}, bf16[512,512]{1,0:T(8,128)(2,1)S(1)}, u32[]{:S(2)}, u32[]{:S(2)}) collective-permute-start(bf16[512,512]{1,0:T(8,128)(2,1)} %get-tuple-element.92), channel_id=1, source_target_pairs={{0,1},{1,0},{2,3},{3,2},{4,5},{5,4},{6,7},{7,6},{8,9},{9,8},{10,11... | collective-permute-start | bytes 1572872 | tf_op jit(solution)/shard_map/ppermute | solution.py:33
  22.0 13.8 %collective-permute-start.3 = (bf16[512,512]{1,0:T(8,128)(2,1)}, bf16[512,512]{1,0:T(8,128)(2,1)S(1)}, u32[]{:S(2)}, u32[]{:S(2)}) collective-permute-start(bf16[512,512]{1,0:T(8,128)(2,1)} %get-tuple-element.93), channel_id=1, source_target_pairs={{0,2},{1,3},{2,0},{3,1},{4,6},{5,7},{6,4},{7,5},{8,10},{9,11},{10,... | collective-permute-start | bytes 1572872 | tf_op jit(solution)/shard_map/ppermute | solution.py:33
  23.2 26.0 %collective-permute-start.4 = (bf16[512,512]{1,0:T(8,128)(2,1)}, bf16[512,512]{1,0:T(8,128)(2,1)S(1)}, u32[]{:S(2)}, u32[]{:S(2)}) collective-permute-start(bf16[512,512]{1,0:T(8,128)(2,1)} %get-tuple-element.94), channel_id=1, source_target_pairs={{0,4},{1,5},{2,6},{3,7},{4,0},{5,1},{6,2},{7,3},{8,12},{9,13},{10,... | collective-permute-start | bytes 1572872 | tf_op jit(solution)/shard_map/ppermute | solution.py:33
  25.6 23.5 %collective-permute-start.5 = (bf16[512,512]{1,0:T(8,128)(2,1)}, bf16[512,512]{1,0:T(8,128)(2,1)S(1)}, u32[]{:S(2)}, u32[]{:S(2)}) collective-permute-start(bf16[512,512]{1,0:T(8,128)(2,1)} %get-tuple-element.95), channel_id=1, source_target_pairs={{0,8},{1,9},{2,10},{3,11},{4,12},{5,13},{6,14},{7,15},{8,0},{9,1},... | collective-permute-start | bytes 1572872 | tf_op jit(solution)/shard_map/ppermute | solution.py:33
  29.6 19.5 %collective-permute-start.6 = (bf16[512,512]{1,0:T(8,128)(2,1)}, bf16[512,512]{1,0:T(8,128)(2,1)S(1)}, u32[]{:S(2)}, u32[]{:S(2)}) collective-permute-start(bf16[512,512]{1,0:T(8,128)(2,1)} %get-tuple-element.96), channel_id=1, source_target_pairs={{0,16},{1,17},{2,18},{3,19},{4,20},{5,21},{6,22},{7,23},{8,24},{9,... | collective-permute-start | bytes 1572872 | tf_op jit(solution)/shard_map/ppermute | solution.py:33
  30.9 25.2 %collective-permute-start.7 = (bf16[512,512]{1,0:T(8,128)(2,1)}, bf16[512,512]{1,0:T(8,128)(2,1)S(1)}, u32[]{:S(2)}, u32[]{:S(2)}) collective-permute-start(bf16[512,512]{1,0:T(8,128)(2,1)} %get-tuple-element.97), channel_id=1, source_target_pairs={{0,32},{1,33},{2,34},{3,35},{4,36},{5,37},{6,38},{7,39},{8,40},{9,... | collective-permute-start | bytes 1572872 | tf_op jit(solution)/shard_map/ppermute | solution.py:33
  56.1 9.1 %collective-permute-start.8 = (bf16[256,512]{1,0:T(8,128)(2,1)}, bf16[256,512]{1,0:T(8,128)(2,1)S(1)}, u32[]{:S(2)}, u32[]{:S(2)}) collective-permute-start(bf16[256,512]{1,0:T(8,128)(2,1)} %collective-permute-done.refs_0_.refs_16_), channel_id=1, source_target_pairs={{0,64},{1,65},{2,66},{3,67},{4,68},{5,69},{6,70},{7,71},{8,72},{9,... | collective-permute-start | bytes 786440 | tf_op jit(solution)/shard_map/ppermute | solution.py:58
  56.3 8.9 %collective-permute-start.9 = (bf16[256,512]{1,0:T(8,128)(2,1)}, bf16[256,512]{1,0:T(8,128)(2,1)S(1)}, u32[]{:S(2)}, u32[]{:S(2)}) collective-permute-start(bf16[256,512]{1,0:T(8,128)(2,1)} %copy-done.16), channel_id=1, source_target_pairs={{0,200},{1,201},{2,202},{3,203},{4,204},{5,205},{6,206},{7,207},{8... | collective-permute-start | bytes 786440 | tf_op jit(solution)/shard_map/ppermute | solution.py:58
  65.4 12.5 %collective-permute-start.10 = (bf16[512,512]{1,0:T(8,128)(2,1)S(1)}, bf16[512,512]{1,0:T(8,128)(2,1)S(1)}, u32[]{:S(2)}, u32[]{:S(2)}) collective-permute-start(bf16[512,512]{1,0:T(8,128)(2,1)S(1)} %get-tuple-element.160), channel_id=1, source_target_pairs={{0,64},{1,65},{2,66},{3,67},{4,68},{5,69},{6,70},{7,71},{8,72},{9,... | collective-permute-start | bytes 1572872 | tf_op jit(solution)/shard_map/ppermute | solution.py:58
  65.5 14.2 %collective-permute-start.11 = (bf16[512,512]{1,0:T(8,128)(2,1)S(1)}, bf16[512,512]{1,0:T(8,128)(2,1)S(1)}, u32[]{:S(2)}, u32[]{:S(2)}) collective-permute-start(bf16[512,512]{1,0:T(8,128)(2,1)S(1)} %get-tuple-element.159), channel_id=1, source_target_pairs={{0,200},{1,201},{2,202},{3,203},{4,204},{5,205},{6,206},{7,207},{8... | collective-permute-start | bytes 1572872 | tf_op jit(solution)/shard_map/ppermute | solution.py:58
  68.1 24.0 %collective-permute-start.12 = (bf16[512,512]{1,0:T(8,128)(2,1)}, bf16[512,512]{1,0:T(8,128)(2,1)S(1)}, u32[]{:S(2)}, u32[]{:S(2)}) collective-permute-start(bf16[512,512]{1,0:T(8,128)(2,1)} %get-tuple-element.115), channel_id=1, source_target_pairs={{0,4},{1,5},{2,6},{3,7},{4,0},{5,1},{6,2},{7,3},{8,12},{9,13},{10,... | collective-permute-start | bytes 1572872 | tf_op jit(solution)/shard_map/ppermute | solution.py:33
  68.7 23.5 %collective-permute-start.13 = (bf16[512,512]{1,0:T(8,128)(2,1)S(1)}, bf16[512,512]{1,0:T(8,128)(2,1)S(1)}, u32[]{:S(2)}, u32[]{:S(2)}) collective-permute-start(bf16[512,512]{1,0:T(8,128)(2,1)S(1)} %copy-done.25), channel_id=1, source_target_pairs={{0,32},{1,33},{2,34},{3,35},{4,36},{5,37},{6,38},{7,39},{8,40},{9,... | collective-permute-start | bytes 1572872 | tf_op jit(solution)/shard_map/ppermute | solution.py:33
  69.2 24.2 %collective-permute-start.14 = (bf16[512,512]{1,0:T(8,128)(2,1)}, bf16[512,512]{1,0:T(8,128)(2,1)S(1)}, u32[]{:S(2)}, u32[]{:S(2)}) collective-permute-start(bf16[512,512]{1,0:T(8,128)(2,1)} %get-tuple-element.119), channel_id=1, source_target_pairs={{0,2},{1,3},{2,0},{3,1},{4,6},{5,7},{6,4},{7,5},{8,10},{9,11},{10,... | collective-permute-start | bytes 1572872 | tf_op jit(solution)/shard_map/ppermute | solution.py:33
  79.7 13.6 %collective-permute-start.15 = (bf16[512,512]{1,0:T(8,128)(2,1)}, bf16[512,512]{1,0:T(8,128)(2,1)}, u32[]{:S(2)}, u32[]{:S(2)}) collective-permute-start(bf16[512,512]{1,0:T(8,128)(2,1)} %get-tuple-element.120), channel_id=1, source_target_pairs={{0,16},{1,17},{2,18},{3,19},{4,20},{5,21},{6,22},{7,23},{8,24},{9,... | collective-permute-start | bytes 1572872 | tf_op jit(solution)/shard_map/ppermute | solution.py:33
  80.6 12.8 %collective-permute-start.16 = (bf16[512,512]{1,0:T(8,128)(2,1)}, bf16[512,512]{1,0:T(8,128)(2,1)}, u32[]{:S(2)}, u32[]{:S(2)}) collective-permute-start(bf16[512,512]{1,0:T(8,128)(2,1)} %get-tuple-element.121), channel_id=1, source_target_pairs={{0,1},{1,0},{2,3},{3,2},{4,5},{5,4},{6,7},{7,6},{8,9},{9,8},{10,11... | collective-permute-start | bytes 1572872 | tf_op jit(solution)/shard_map/ppermute | solution.py:33
  92.2 20.2 %collective-permute-start.17 = (bf16[768,512]{1,0:T(8,128)(2,1)}, bf16[768,512]{1,0:T(8,128)(2,1)S(1)}, u32[]{:S(2)}, u32[]{:S(2)}) collective-permute-start(bf16[768,512]{1,0:T(8,128)(2,1)} %feature_rows.1.refs_2_), channel_id=1, source_target_pairs={{0,4},{1,5},{2,6},{3,7},{4,0},{5,1},{6,2},{7,3},{8,12},{9,13},{10,... | collective-permute-start | bytes 2359304 | tf_op jit(solution)/shard_map/ppermute | solution.py:33
  92.3 21.5 %collective-permute-start.18 = (bf16[768,512]{1,0:T(8,128)(2,1)}, bf16[768,512]{1,0:T(8,128)(2,1)}, u32[]{:S(2)}, u32[]{:S(2)}) collective-permute-start(bf16[768,512]{1,0:T(8,128)(2,1)} %feature_rows.1.refs_2_), channel_id=1, source_target_pairs={{0,32},{1,33},{2,34},{3,35},{4,36},{5,37},{6,38},{7,39},{8,40},{9,... | collective-permute-start | bytes 2359304 | tf_op jit(solution)/shard_map/ppermute | solution.py:33
  93.4 32.6 %collective-permute-start.19 = (bf16[768,512]{1,0:T(8,128)(2,1)}, bf16[768,512]{1,0:T(8,128)(2,1)}, u32[]{:S(2)}, u32[]{:S(2)}) collective-permute-start(bf16[768,512]{1,0:T(8,128)(2,1)} %feature_rows.1.refs_2_), channel_id=1, source_target_pairs={{0,2},{1,3},{2,0},{3,1},{4,6},{5,7},{6,4},{7,5},{8,10},{9,11},{10,... | collective-permute-start | bytes 2359304 | tf_op jit(solution)/shard_map/ppermute | solution.py:33
  93.5 36.0 %collective-permute-start.20 = (bf16[768,512]{1,0:T(8,128)(2,1)}, bf16[768,512]{1,0:T(8,128)(2,1)}, u32[]{:S(2)}, u32[]{:S(2)}) collective-permute-start(bf16[768,512]{1,0:T(8,128)(2,1)} %feature_rows.1.refs_2_), channel_id=1, source_target_pairs={{0,16},{1,17},{2,18},{3,19},{4,20},{5,21},{6,22},{7,23},{8,24},{9,... | collective-permute-start | bytes 2359304 | tf_op jit(solution)/shard_map/ppermute | solution.py:33
  94.4 35.1 %collective-permute-start.21 = (bf16[768,512]{1,0:T(8,128)(2,1)}, bf16[768,512]{1,0:T(8,128)(2,1)}, u32[]{:S(2)}, u32[]{:S(2)}) collective-permute-start(bf16[768,512]{1,0:T(8,128)(2,1)} %feature_rows.1.refs_2_), channel_id=1, source_target_pairs={{0,1},{1,0},{2,3},{3,2},{4,5},{5,4},{6,7},{7,6},{8,9},{9,8},{10,11... | collective-permute-start | bytes 2359304 | tf_op jit(solution)/shard_map/ppermute | solution.py:33
  129.5 21.9 %collective-permute-start.22 = (bf16[768,512]{1,0:T(8,128)(2,1)}, bf16[768,512]{1,0:T(8,128)(2,1)S(1)}, u32[]{:S(2)}, u32[]{:S(2)}) collective-permute-start(bf16[768,512]{1,0:T(8,128)(2,1)} %get-tuple-element.134.refs_2_), channel_id=1, source_target_pairs={{0,1},{1,0},{2,3},{3,2},{4,5},{5,4},{6,7},{7,6},{8,9},{9,8},{10,11... | collective-permute-start | bytes 2359304 | tf_op jit(solution)/shard_map/ppermute | solution.py:33
  140.4 10.2 %collective-permute-start.28 = (bf16[256,512]{1,0:T(8,128)(2,1)S(1)}, bf16[256,512]{1,0:T(8,128)(2,1)S(1)}, u32[]{:S(2)}, u32[]{:S(2)}) collective-permute-start(bf16[256,512]{1,0:T(8,128)(2,1)S(1)} %slice.6), channel_id=1, source_target_pairs={{0,64},{1,65},{2,66},{3,67},{4,68},{5,69},{6,70},{7,71},{8,72},{9,... | collective-permute-start | bytes 786440 | tf_op jit(solution)/shard_map/ppermute | solution.py:58
  140.6 19.4 %collective-permute-start.24 = (bf16[768,512]{1,0:T(8,128)(2,1)S(1)}, bf16[768,512]{1,0:T(8,128)(2,1)S(1)}, u32[]{:S(2)}, u32[]{:S(2)}) collective-permute-start(bf16[768,512]{1,0:T(8,128)(2,1)S(1)} %copy-done.17), channel_id=1, source_target_pairs={{0,2},{1,3},{2,0},{3,1},{4,6},{5,7},{6,4},{7,5},{8,10},{9,11},{10,... | collective-permute-start | bytes 2359304 | tf_op jit(solution)/shard_map/ppermute | solution.py:33
  140.7 40.9 %collective-permute-start.26 = (bf16[768,512]{1,0:T(8,128)(2,1)S(1)}, bf16[768,512]{1,0:T(8,128)(2,1)S(1)}, u32[]{:S(2)}, u32[]{:S(2)}) collective-permute-start(bf16[768,512]{1,0:T(8,128)(2,1)S(1)} %copy-done.17), channel_id=1, source_target_pairs={{0,16},{1,17},{2,18},{3,19},{4,20},{5,21},{6,22},{7,23},{8,24},{9,... | collective-permute-start | bytes 2359304 | tf_op jit(solution)/shard_map/ppermute | solution.py:33
  140.8 40.9 %collective-permute-start.25 = (bf16[768,512]{1,0:T(8,128)(2,1)S(1)}, bf16[768,512]{1,0:T(8,128)(2,1)}, u32[]{:S(2)}, u32[]{:S(2)}) collective-permute-start(bf16[768,512]{1,0:T(8,128)(2,1)S(1)} %copy-done.17), channel_id=1, source_target_pairs={{0,4},{1,5},{2,6},{3,7},{4,0},{5,1},{6,2},{7,3},{8,12},{9,13},{10,... | collective-permute-start | bytes 2359304 | tf_op jit(solution)/shard_map/ppermute | solution.py:33
  150.6 31.0 %collective-permute-start.27 = (bf16[768,512]{1,0:T(8,128)(2,1)S(1)}, bf16[768,512]{1,0:T(8,128)(2,1)}, u32[]{:S(2)}, u32[]{:S(2)}) collective-permute-start(bf16[768,512]{1,0:T(8,128)(2,1)S(1)} %copy-done.17), channel_id=1, source_target_pairs={{0,32},{1,33},{2,34},{3,35},{4,36},{5,37},{6,38},{7,39},{8,40},{9,... | collective-permute-start | bytes 2359304 | tf_op jit(solution)/shard_map/ppermute | solution.py:33
  158.3 13.8 %collective-permute-start.23 = (bf16[256,512]{1,0:T(8,128)(2,1)}, bf16[256,512]{1,0:T(8,128)(2,1)}, u32[]{:S(2)}, u32[]{:S(2)}) collective-permute-start(bf16[256,512]{1,0:T(8,128)(2,1)} %get-tuple-element.135), channel_id=1, source_target_pairs={{0,8},{1,9},{2,10},{3,11},{4,12},{5,13},{6,14},{7,15},{8,0},{9,1},... | collective-permute-start | bytes 786440 | tf_op jit(solution)/shard_map/ppermute | solution.py:33
  159.9 21.7 %collective-permute-start.29 = (bf16[256,512]{1,0:T(8,128)(2,1)S(1)}, bf16[256,512]{1,0:T(8,128)(2,1)S(1)}, u32[]{:S(2)}, u32[]{:S(2)}) collective-permute-start(bf16[256,512]{1,0:T(8,128)(2,1)S(1)} %collective-permute-done.28.refs_17_), channel_id=1, source_target_pairs={{0,64},{1,65},{2,66},{3,67},{4,68},{5,69},{6,70},{7,71},{8,72},{9,... | collective-permute-start | bytes 786440 | tf_op jit(solution)/shard_map/ppermute | solution.py:58
  172.2 9.5 %collective-permute-start.31 = (bf16[256,512]{1,0:T(8,128)(2,1)S(1)}, bf16[256,512]{1,0:T(8,128)(2,1)}, u32[]{:S(2)}, u32[]{:S(2)}) collective-permute-start(bf16[256,512]{1,0:T(8,128)(2,1)S(1)} %collective-permute-done.30.refs_20_), channel_id=1, source_target_pairs={{0,200},{1,201},{2,202},{3,203},{4,204},{5,205},{6,206},{7,207},{8... | collective-permute-start | bytes 786440 | tf_op jit(solution)/shard_map/ppermute | solution.py:58
  (27 other events, 508.1 us)
Sparse Core Ops, SparseCore 0:
  65.4 55.0 all-gather.1
